TPU v7x, 256 devices: a whole 4x4x8 slice. The times are simulated.
256 devices in a mesh: expert: 64 (over x, z, core), et: 4 (over y).
Axes of the slice: x: 4, y: 4, z: 8, core: 2. Of those that a mesh axis runs over, the one named last changes fastest.
Arguments:
- grad_out: bfloat16 [8192, 3584], P('expert', 'et'), may hold values from -0.59765625 to 0.59765625
- routing: int32 [8192, 8], P('expert'), may hold values from 0 to 127, all different within a row; in each aligned block of 128 rows (0 to 127, 128 to 255, ...) at most 16 rows name the same one
- gates: float32 [8192, 8], P('expert'), may hold values from 0.1 to 1
- hidden: bfloat16 [128, 1024, 1024], P('expert', None, 'et'), may hold values from -42 to 42, as said below
- momentum: bfloat16 [128, 3584, 1024], P('expert', None, 'et'), may hold values from -6 to 6
- right_factor: float32 [128, 32, 1024], P('expert', None, 'et'), may hold values from -0.1875 to 0.1875
Outputs:
- new_momentum: bfloat16 [128, 3584, 1024], P('expert', None, 'et')
- left_factor: float32 [128, 32, 3584], P('expert')
- new_right: float32 [128, 32, 1024], P('expert', None, 'et')
Inputs may be any that keep to these rules, and one draw needn't show every extreme that they name: `routing`: each row names 8 different experts; among the 128 rows of one index of expert no expert is named more than 16 times, a bound that some block reaches. `hidden`: slots that no token fills hold arbitrary values.
All inputs are finite; a program needn't handle non-finite values.
Results may differ from a plain program's by a relative error of at most 0.0048.
Values may be sent and summed in bfloat16 or wider, within the bound.
No kernel may reach another device: no remote copies, remote signals or barrier semaphores. Data moves between devices by JAX's collectives and lax.ppermute only.
A program may use at most 128 MiB of HBM per device.

v0:
```python
import jax
import jax.numpy as jnp
from jax import lax
from jax.sharding import PartitionSpec as P

momentum_decay = 0.95
epsilon = 1e-06


def body(grad_out, routing, gates, hidden, momentum, right_factor):
    highest = lax.Precision.HIGHEST
    local_count = hidden.shape[0]
    slot_count = hidden.shape[1]
    owners = lax.axis_size("expert")
    capacity = slot_count // owners
    experts = local_count * owners
    tok_rows = routing.shape[0]
    choices_each = routing.shape[1]
    routes_flat = routing.reshape(-1)
    one_hot = (routes_flat[:, None] == jnp.arange(experts, dtype=jnp.int32)[None, :]).astype(
        jnp.int32
    )
    before = jnp.cumsum(one_hot, axis=0) - one_hot
    slot_index = jnp.sum(before * one_hot, axis=1)
    target = (
        routes_flat % local_count * owners + routes_flat // local_count
    ) * capacity + slot_index
    token_of = jnp.arange(tok_rows * choices_each, dtype=jnp.int32) // choices_each
    row_gates = gates.reshape(-1)[:, None]
    full_columns = lax.all_gather(grad_out, "et", axis=1, tiled=True)
    width = full_columns.shape[1]
    scaled = (full_columns[token_of].astype(jnp.float32) * row_gates).astype(jnp.bfloat16)
    send_buffer = (
        jnp.zeros((local_count * owners * capacity, width), jnp.bfloat16).at[target].set(scaled)
    )
    send_buffer = send_buffer.reshape(local_count, owners, capacity, width)
    arrived = lax.all_to_all(send_buffer, "expert", split_axis=1, concat_axis=1, tiled=True)
    arrived = arrived.reshape(local_count, slot_count, arrived.shape[3])
    gradient = jnp.einsum("esd,esh->edh", arrived, hidden, preferred_element_type=jnp.float32)
    buffer = momentum.astype(jnp.float32) + gradient
    partial_value = jnp.einsum(
        "erh,edh->erd", right_factor, buffer, precision=highest, preferred_element_type=jnp.float32
    )
    solve_rows = jax.vmap(
        lambda factor, rows: jax.scipy.linalg.solve_triangular(factor, rows, lower=True)
    )
    projected = lax.psum(partial_value, "et")
    gram_matrix = jnp.einsum(
        "erd,esd->ers", projected, projected, precision=highest, preferred_element_type=jnp.float32
    )
    cholesky_factor = jnp.linalg.cholesky(gram_matrix)
    left_factor = solve_rows(cholesky_factor, projected)
    raw_right = jnp.einsum(
        "erd,edh->erh", left_factor, buffer, precision=highest, preferred_element_type=jnp.float32
    )
    update = jnp.einsum(
        "erd,erh->edh",
        left_factor,
        raw_right,
        precision=highest,
        preferred_element_type=jnp.float32,
    )
    new_momentum = (buffer - (1.0 - momentum_decay) * update).astype(jnp.bfloat16)
    column_sums = lax.psum(jnp.sum(raw_right * raw_right, axis=2, keepdims=True), "et")
    new_right = raw_right / jnp.sqrt(column_sums + epsilon)
    return (new_momentum, left_factor, new_right)


def solution(mesh):
    placed = (
        P("expert", "et"),
        P("expert", None),
        P("expert", None),
        P("expert", None, "et"),
        P("expert", None, "et"),
        P("expert", None, "et"),
    )
    return jax.shard_map(
        body,
        mesh=mesh,
        in_specs=placed,
        out_specs=(P("expert", None, "et"), P("expert", None, None), P("expert", None, "et")),
        check_vma=False,
    )
```

profile of v0, /device:TPU:2, one launch (start us, length us, event | category | flops | bytes accessed | tf_op | source)
XLA Modules:
  0.0 522.8 jit_solution(2550141945438324757)
XLA Ops:
  7.2 0.9 copy.31
  8.1 0.1 eq.31
  8.2 0.1 eq.27
  8.3 0.1 reshape.207
  8.4 0.1 copy.34
  8.5 0.2 fusion.4
  8.8 0.1 copy.35
  8.9 14.9 %all_gather.3 = bf16[128,3584]{1,0:T(8,128)(2,1)S(1)} all-gather(bf16[128,896]{1,0:T(8,128)(2,1)} %param.6), channel_id=1, replica_groups=mesh['expert'=64,'et'=4] {'et'}, dimensions={1}, use_global_device_ids=true | all-gather | bytes 1146880 | tf_op jit(solution)/shard_map/all_gather | solution.py:30
  23.8 0.8 copy.36
  24.6 0.1 mul.53
  24.7 0.4 fusion.3
  25.1 7.3 %gather_fusion = bf16[1024,3584]{1,0:T(8,128)(2,1)} fusion(bf16[128,3584]{1,0:T(8,128)(2,1)S(1)} %all_gather.3, s32[1024]{0:T(1024)S(1)} %broadcast_clamp_fusion), kind=kCustom, calls=%fused_computation | custom fusion | bytes 14684160 | tf_op jit(solution)/shard_map/gather | solution.py:32
  32.4 8.5 %multiply_convert_fusion = bf16[1024,3584]{1,0:T(8,128)(2,1)} fusion(bf16[1024,3584]{1,0:T(8,128)(2,1)} %gather_fusion, f32[1024]{0:T(1024)S(1)} %mul.53), kind=kLoop, calls=%fused_computation.2 | loop fusion | flops 11010048 | bytes 14684160 | tf_op jit(solution)/shard_map/convert_element_type | solution.py:32
  40.9 19.6 %scatter_custom_fusion = bf16[2048,3584]{1,0:T(8,128)(2,1)} fusion(s32[1024]{0:T(1024)S(1)} %bitcast.45, bf16[1024,3584]{1,0:T(8,128)(2,1)} %multiply_convert_fusion, bf16[]{:T(256)} %constant.88.clone.1), kind=kCustom, calls=%fused_computation.4 | custom fusion | bytes 14680576 | tf_op jit(solution)/shard_map/scatter | solution.py:34
  60.5 7.6 %copy.37 = bf16[2,64,16,3584]{3,2,0,1:T(8,128)(2,1)S(1)} copy(bf16[2,64,16,3584]{3,2,1,0:T(8,128)(2,1)} %bitcast.40) | data formatting | bytes 29360128 | tf_op jit(solution)/shard_map/reshape | solution.py:36
  68.1 331.0 %all_to_all.5 = bf16[2,64,16,3584]{3,2,0,1:T(8,128)(2,1)S(1)} all-to-all(bf16[2,64,16,3584]{3,2,0,1:T(8,128)(2,1)S(1)} %copy.37), channel_id=1, replica_groups=mesh['expert'=64,'et'=4] {'expert'}, dimensions={1} | all-to-all | bytes 29360128 | tf_op jit(solution)/shard_map/all_to_all | solution.py:37
  399.1 6.5 %copy.38 = bf16[2,64,16,3584]{3,2,1,0:T(8,128)(2,1)} copy(bf16[2,64,16,3584]{3,2,0,1:T(8,128)(2,1)S(1)} %all_to_all.5) | data formatting | bytes 29360128 | tf_op jit(solution)/shard_map/all_to_all | solution.py:37
  405.6 9.1 %convert_add_fusion = f32[2,3584,256]{2,1,0:T(8,128)S(1)} fusion(bf16[2,3584,256]{2,1,0:T(8,128)(2,1)S(1)} %copy-done.4, bf16[2,1024,3584]{2,1,0:T(8,128)(2,1)} %bitcast.41, bf16[2,1024,256]{2,1,0:T(8,128)(2,1)S(1)} %copy-done), kind=kOutput, calls=%fused_computation.6 | convolution fusion | flops 3761766400 | bytes 26738688 | tf_op jit(solution)/shard_map/esd,esh->edh/dot_general | solution.py:39
  414.7 3.0 copy-done.1
  417.7 7.7 %convolution_bitcast_fusion = f32[2,32,3584]{2,1,0:T(8,128)} fusion(f32[2,3584,256]{2,1,0:T(8,128)S(1)} %convert_add_fusion, f32[2,32,256]{2,1,0:T(8,128)S(1)} %copy-done.3), kind=kOutput, calls=%fused_computation.7 | convolution fusion | flops 704643072 | bytes 8323072 | tf_op jit(solution)/shard_map/erh,edh->erd/dot_general | solution.py:41
  425.4 48.8 %all-reduce.2.cloned.1.call-done = f32[2,32,3584]{2,1,0:T(8,128)} async-done(((f32[2,32,3584]{2,1,0:T(8,128)}), f32[2,32,3584]{2,1,0:T(8,128)}) %all-reduce.2.cloned.1.call-update) | async-done | bytes 917520 | tf_op jit(solution)/shard_map/psum | solution.py:47
  474.2 2.4 fusion.12
  476.6 0.1 copy.40
  476.7 5.9 %custom-call.8 = f32[2,32,32]{2,1,0:T(8,128)S(1)} custom-call(f32[2,32,32]{2,1,0:T(8,128)S(1)} %fusion.9), custom_call_target="Cholesky" | custom-call | tf_op jit(solution)/shard_map/jit(cholesky)/cholesky | solution.py:51
  482.6 0.1 compare_reduce_fusion
  482.7 0.1 select_bitcast_fusion
  482.8 4.9 custom-call.9
  487.7 2.1 fusion.7
  489.9 6.2 %multiply_reduce_fusion = (f32[2,32]{1,0:T(2,128)S(1)}, f32[2,32,256]{2,1,0:T(8,128)S(1)}) fusion(f32[2,32,3584]{2,1,0:T(8,128)S(1)} %fusion.7, f32[2,3584,256]{2,1,0:T(8,128)} %copy-done.1), kind=kOutput, calls=%fused_computation.17 | convolution fusion | flops 704675776 | bytes 8323328 | tf_op jit(solution)/shard_map/erd,edh->erh/dot_general | solution.py:53
  496.1 9.7 %psum.15 = f32[2,32,1]{1,0,2:T(2,128)S(1)} all-reduce(f32[2,32,1]{1,0,2:T(2,128)S(1)} %bitcast.44), channel_id=1, replica_groups=mesh['expert'=64,'et'=4] {'et'}, use_global_device_ids=true, to_apply=%region_8.9 | all-reduce | flops 64 | bytes 512 | tf_op jit(solution)/shard_map/psum | solution.py:64
  505.8 9.4 %subtract_convert_fusion = bf16[2,3584,256]{2,1,0:T(8,128)(2,1)} fusion(f32[2,3584,256]{2,1,0:T(8,128)} %copy-done.1, f32[2,32,3584]{2,1,0:T(8,128)S(1)} %fusion.7, f32[2,32,256]{2,1,0:T(8,128)S(1)} %get-tuple-element.4), kind=kOutput, calls=%fused_computation.3 | convolution fusion | flops 710148096 | bytes 11993088 | tf_op jit(solution)/shard_map/erd,erh->edh/dot_general | solution.py:56
  515.2 0.7 broadcast_divide_fusion
  (23 shorter events, 0.3 us)
Async XLA Ops:
  7.2 398.5 %copy-start = (bf16[2,1024,256]{2,1,0:T(8,128)(2,1)S(1)}, bf16[2,1024,256]{2,1,0:T(8,128)(2,1)}, u32[]{:S(2)}) copy-start(bf16[2,1024,256]{2,1,0:T(8,128)(2,1)} %param.9) | copy-start | bytes 3145732
  7.2 467.0 %all-reduce.2.cloned.1.call-start = ((), (), s32[]{:S(2)}) async-start(), calls=%async_computation.1 | async-start | bytes 1835008 | tf_op jit(solution)/shard_map/psum | solution.py:47
  399.1 6.5 %copy-start.4 = (bf16[2,3584,256]{2,1,0:T(8,128)(2,1)S(1)}, bf16[2,3584,256]{2,1,0:T(8,128)(2,1)}, u32[]{:S(2)}) copy-start(bf16[2,3584,256]{2,1,0:T(8,128)(2,1)} %param.10) | copy-start | bytes 11010052
  405.6 12.1 %copy-start.3 = (f32[2,32,256]{2,1,0:T(8,128)S(1)}, f32[2,32,256]{2,1,0:T(8,128)}, u32[]{:S(2)}) copy-start(f32[2,32,256]{2,1,0:T(8,128)} %param.11) | copy-start | bytes 196612
  414.7 3.0 copy-start.1
  489.8 25.4 %copy-start.2 = (f32[2,32,3584]{2,1,0:T(8,128)}, f32[2,32,3584]{2,1,0:T(8,128)S(1)}, u32[]{:S(2)}) copy-start(f32[2,32,3584]{2,1,0:T(8,128)S(1)} %fusion.7) | copy-start | bytes 2752516
Sparse Core Ops, SparseCore 0:
  425.5 48.6 all-reduce.1
where the time goes:
time: 523 us
  blocking collectives  356 us (68%)
  waiting for transfers between devices  48.8 us (9%)
  local copies, waits for them, and re-layouts  46.3 us (9%)
  matrix products  36.9 us (7%)
  other arithmetic  20.9 us (4%)
  between operations  14.2 us (3%)
    all_to_all x1, blocking collectives, body(): lax.all_to_all(send_buffer, 'expert', split_axis=1, concat_axis=1, tiled=...  331 us
    psum x1, waiting for transfers between devices, body(): projected = lax.psum(partial_value, 'et')  48.8 us
    scatter x1, local copies, waits for them, and re-layouts, body(): jnp.zeros((local_count * owners * capacity, width), jnp.bfloat16).at[target]  19.6 us
    all_gather x1, blocking collectives, body(): full_columns = lax.all_gather(grad_out, 'et', axis=1, tiled=True)  14.9 us
  transfers between devices with their start and end apart: 1, of which 1 were waited for; matrix products, arithmetic and copies ran while one was open for 0% of the time, Pallas kernels for 0%

commit v1 on v0

v1 whole, which is shorter than its diff:
```python
import functools

import functools

import jax
import jax.numpy as jnp
from jax import lax
from jax.experimental import pallas as pl
from jax.experimental.pallas import tpu as pltpu
from jax.sharding import PartitionSpec as P

momentum_decay = 0.95
epsilon = 1e-06
HIGHEST = lax.Precision.HIGHEST
f32 = jnp.float32
bf16 = jnp.bfloat16
CHUNKS = ((0, 1, -1), (2, -2, 3, -3, 4))
META = 16


def ring(size, step):
    return [(i, (i + step) % size) for i in range(size)]


def thirds(x):
    high = x.astype(bf16)
    rest = x - high.astype(f32)
    middle = rest.astype(bf16)
    return high, middle, (rest - middle.astype(f32)).astype(bf16)


def call(kernel, out_shape, cost, **more):
    flops, moved = cost
    return pl.pallas_call(
        kernel,
        grid=(1,),
        out_shape=out_shape,
        compiler_params=pltpu.CompilerParams(vmem_limit_bytes=20 * 1024 * 1024),
        cost_estimate=pl.CostEstimate(flops=flops, bytes_accessed=moved, transcendentals=0),
        **more,
    )


def whole(shape):
    return pl.BlockSpec(shape, lambda i: (0,) * len(shape))


def of_expert(j, shape):
    return pl.BlockSpec((None,) + tuple(shape), lambda i: (j,) + (0,) * len(shape))


def rows_of(ref):
    members, steps, capacity, width = ref.shape
    return ref[...].reshape(members * steps * capacity, width)


def project_kernel(chunks, weights_ref, old_ref, *refs):
    arrived, out_ref = refs[:chunks], refs[-1]
    rank = old_ref.shape[0]
    stacked = jnp.concatenate(thirds(weights_ref[...]), axis=0)
    total = old_ref[...]
    at = 0
    for ref in arrived:
        block = rows_of(ref)
        slots = block.shape[0]
        sums = jnp.dot(stacked[:, at : at + slots], block, preferred_element_type=f32)
        total = total + (sums[:rank] + (sums[rank : 2 * rank] + sums[2 * rank :]))
        at += slots
    out_ref[...] = total


def gradient_kernel(chunks, count, *refs):
    arrived, refs = [rows_of(ref) for ref in refs[:chunks]], refs[chunks:]
    for hidden_ref, out_ref in zip(refs[:count], refs[-count:]):
        total = None
        at = 0
        for block in arrived:
            slots = block.shape[0]
            product = lax.dot_general(
                block,
                hidden_ref[at : at + slots],
                (((0,), (0,)), ((), ())),
                preferred_element_type=f32,
            )
            total = product if total is None else total + product
            at += slots
        out_ref[...] = total.astype(bf16)


def right_kernel(me_ref, left_ref, momentum_ref, *refs):
    grads, out_ref = refs[:-1], refs[-1]
    quarters, rank, width = left_ref.shape
    total = jnp.zeros(out_ref.shape, f32)
    for d, grad_ref in enumerate(grads):
        at = lax.rem(me_ref[0] + d, quarters)
        stacked = jnp.concatenate(thirds(left_ref[at]), axis=0)
        sums = jnp.dot(stacked, momentum_ref[at], preferred_element_type=f32) + jnp.dot(
            stacked, grad_ref[...], preferred_element_type=f32
        )
        total = total + (sums[:rank] + (sums[rank : 2 * rank] + sums[2 * rank :]))
    out_ref[...] = total


def update_kernel(me_ref, left_ref, raw_ref, momentum_ref, *refs):
    out_ref = refs[-1]
    quarters = left_ref.shape[0]
    raw_high, raw_low, _ = thirds((1.0 - momentum_decay) * raw_ref[...])
    raw = jnp.concatenate([raw_high, raw_low, raw_high], axis=0)
    for d in range(quarters):
        at = lax.rem(me_ref[0] + d, quarters)
        high, low, _ = thirds(left_ref[at])
        left = jnp.concatenate([high, high, low], axis=0)
        update = lax.dot_general(
            left, raw, (((0,), (0,)), ((), ())), preferred_element_type=f32
        )
        buffer = momentum_ref[at].astype(f32) + refs[d][...].astype(f32)
        out_ref[at] = (buffer - update).astype(bf16)


def passing_kernel(*refs):
    pass


def passing(values, awaited):
    anywhere = pl.BlockSpec(memory_space=pl.ANY)
    return pl.pallas_call(
        passing_kernel,
        out_shape=[jax.ShapeDtypeStruct(value.shape, value.dtype) for value in values],
        in_specs=[anywhere] * (len(values) + len(awaited)),
        out_specs=[anywhere] * len(values),
        input_output_aliases={i: i for i in range(len(values))},
        cost_estimate=pl.CostEstimate(flops=0, bytes_accessed=0, transcendentals=0),
    )(*values, *awaited)


def pack_kernel(tokens_ref, routing_ref, gates_ref, out_ref):
    rows = tokens_ref.shape[0]
    high, middle, low = (part.astype(f32) for part in thirds(gates_ref[...]))
    out_ref[:rows] = tokens_ref[...]
    out_ref[rows:] = jnp.zeros((META, out_ref.shape[1]), bf16)
    first = jnp.concatenate([routing_ref[...].astype(f32), high], axis=0)
    out_ref[rows:, 0:rows] = first.astype(bf16)
    out_ref[rows:, rows : 2 * rows] = jnp.concatenate([middle, low], axis=0).astype(bf16)


def order_kernel(place_ref, hidden_ref, right_ref, *outs):
    local, along_x, along_z, cores, capacity, cols = hidden_ref.shape
    for j in range(local):
        at = 0
        for steps in CHUNKS:
            for x in range(along_x):
                for c in range(cores):
                    for k in steps:
                        z = lax.rem(place_ref[0] - k + along_z, along_z)
                        outs[j][at : at + capacity] = hidden_ref[j, x, z, c]
                        at += capacity
        outs[j][at:] = jnp.concatenate(thirds(right_ref[j]), axis=0)


def old_kernel(right_ref, momentum_ref, out_ref):
    local, rank = right_ref.shape[:2]
    for j in range(local):
        stacked = jnp.concatenate(thirds(right_ref[j]), axis=0)
        sums = lax.dot_general(
            stacked, momentum_ref[j], (((1,), (1,)), ((), ())), preferred_element_type=f32
        )
        out_ref[j] = sums[:rank] + (sums[rank : 2 * rank] + sums[2 * rank :])


def factor_kernel(me_ref, *refs):
    parts, out_ref = refs[:-1], refs[-1]
    quarters, rank, width = out_ref.shape
    gram = jnp.zeros((rank, rank), f32)
    for ref in parts:
        gram = gram + lax.dot_general(
            ref[...], ref[...], (((1,), (1,)), ((), ())), precision=HIGHEST, preferred_element_type=f32
        )
    row = lax.broadcasted_iota(jnp.int32, (rank, rank), 0)
    column = lax.broadcasted_iota(jnp.int32, (rank, rank), 1)
    below = lax.broadcasted_iota(jnp.int32, (rank, 1), 0)
    table = jnp.concatenate([gram, (row == column).astype(f32)], axis=1)
    scale = jnp.zeros((rank, 1), f32)
    for k in range(rank):
        pivot = table[k : k + 1, k : k + 1]
        scale = jnp.where(below == k, lax.rsqrt(pivot), scale)
        if k + 1 < rank:
            ratio = jnp.where(below > k, table[:, k : k + 1] / pivot, 0.0)
            table = table - ratio * table[k : k + 1, :]
    inverse = scale * table[:, rank:]
    for d, ref in enumerate(parts):
        at = lax.rem(me_ref[0] - d + quarters, quarters)
        out_ref[at] = jnp.dot(inverse, ref[...], precision=HIGHEST, preferred_element_type=f32)


def weigh_kernel(count, *refs):
    out_ref = refs[-1]
    rank, slots = out_ref.shape
    total = jnp.zeros(out_ref.shape, f32)
    for ref in refs[:count]:
        sums = lax.dot_general(
            ref[slots:], ref[:slots], (((1,), (1,)), ((), ())), preferred_element_type=f32
        )
        total = total + (sums[:rank] + (sums[rank : 2 * rank] + sums[2 * rank :]))
    out_ref[...] = total


def slots_kernel(parts, chosen_experts, local, place_ref, *refs):
    out_ref = refs[-1]
    targets, count, _, capacity, width = out_ref.shape
    rows = 128
    pairs = count * targets
    number = lax.broadcasted_iota(jnp.int32, (pairs, 1), 0)
    member = number % targets
    expert = (
        chosen_experts[0] + number // targets
        + local * (member % 2)
        + 2 * local * place_ref[0]
        + 2 * local * 8 * (member // 2)
    ).astype(f32)
    earlier = (
        lax.broadcasted_iota(jnp.int32, (rows, rows), 0)
        < lax.broadcasted_iota(jnp.int32, (rows, rows), 1)
    ).astype(f32).astype(bf16)
    slot = lax.broadcasted_iota(jnp.int32, (pairs, capacity, rows), 1).astype(f32)
    at = 0
    for n, pieces in enumerate(parts):
        block = refs[at][...]
        if pieces > 1:
            block = jnp.concatenate([refs[at + i][...] for i in range(pieces)], axis=0)
        at += pieces
        first = block[rows:, 0:rows].astype(f32)
        second = block[rows:, rows : 2 * rows].astype(f32)
        gates = first[8:] + (second[:8] + second[8:])
        chosen = jnp.zeros((pairs, rows), f32)
        gate_of = jnp.zeros((pairs, rows), f32)
        for k in range(8):
            match = first[k : k + 1] == expert
            chosen = jnp.where(match, 1.0, chosen)
            gate_of = jnp.where(match, gates[k : k + 1], gate_of)
        rank = jnp.dot(chosen.astype(bf16), earlier, preferred_element_type=f32)
        place = jnp.where(chosen > 0.0, rank, -1.0)
        picked = place[:, None, :] == slot
        row_gate = jnp.sum(jnp.where(picked, gate_of[:, None, :], 0.0), axis=2, keepdims=True)
        flat = jnp.where(picked, 1.0, 0.0).reshape(pairs * capacity, rows).astype(bf16)
        values = jnp.dot(flat, block[:rows], preferred_element_type=f32)
        scaled = (values * row_gate.reshape(pairs * capacity, 1)).astype(bf16)
        for j in range(count):
            for target in range(targets):
                start = (j * targets + target) * capacity
                out_ref[target, j, n] = scaled[start : start + capacity]


def body(grad_out, routing, gates, hidden, momentum, right_factor):
    local, slot_count, cols = hidden.shape
    owners = lax.axis_size("expert")
    quarters = lax.axis_size("et")
    me = lax.axis_index("et")
    capacity = slot_count // owners
    rows, width = grad_out.shape
    depth = momentum.shape[1]
    rank = right_factor.shape[1]
    along_x, along_z, cores = 4, 8, 2
    members = along_x * cores
    scalar = me.astype(jnp.int32).reshape(1)
    z_place = (lax.axis_index("expert") // cores % along_z).astype(jnp.int32).reshape(1)
    blocks_of = momentum.reshape(local, quarters, width, cols)
    smem = pl.BlockSpec(memory_space=pltpu.SMEM)

    def device(x, z, c):
        return (x * along_z + z % along_z) * cores + c

    def z_shift(value, step):
        return lax.ppermute(
            value,
            "expert",
            [
                (device(x, z, c), device(x, z + step, c))
                for x in range(along_x)
                for z in range(along_z)
                for c in range(cores)
            ],
        )

    planes = [
        [device(x, z, c) for x in range(along_x) for c in range(cores)] for z in range(along_z)
    ]

    packed = call(
        pack_kernel,
        jax.ShapeDtypeStruct((rows + META, width), bf16),
        (0, 4 * rows * width),
    )(grad_out, routing.T, gates.T)
    ordered = call(
        order_kernel,
        [jax.ShapeDtypeStruct((slot_count + 3 * rank, cols), bf16)] * local,
        (0, 4 * local * slot_count * cols),
        in_specs=[
            smem,
            whole((local, along_x, along_z, cores, capacity, cols)),
            whole(right_factor.shape),
        ],
        out_specs=[whole((slot_count + 3 * rank, cols))] * local,
    )(z_place, hidden.reshape(local, along_x, along_z, cores, capacity, cols), right_factor)
    held = [
        [ordered[j]] + [lax.ppermute(ordered[j], "et", ring(quarters, d)) for d in range(1, quarters)]
        for j in range(local)
    ]
    old = call(
        old_kernel,
        jax.ShapeDtypeStruct((local, rank, depth), f32),
        (6 * local * rank * cols * depth, 2 * local * depth * cols),
    )(right_factor, momentum)
    partial = old
    old = lax.psum_scatter(partial, "et", scatter_dimension=2, tiled=True)

    blocks = {0: [packed]}
    up = down = packed
    first, last = held
    gates_at = {1: first[1::2], 2: last[1::2], 3: first[2:3]}
    for k in range(1, along_z // 2):
        up, down = z_shift(up, 1), z_shift(down, -1)
        blocks[k], blocks[-k] = [up], [down]
        if k in gates_at:
            up, down = passing((up, down), gates_at[k])
    half = 80
    blocks[along_z // 2] = [z_shift(up[:half], 1), z_shift(down[half:], -1)]

    plan = [(CHUNKS[0], tuple(range(local)), [partial])]
    plan += [(CHUNKS[1], (0,), []), (CHUNKS[1], (1,), [old])]
    arrivals = [[] for _ in range(local)]
    sent = ordered[0]
    for steps, chosen, awaited in plan:
        awaited = awaited + [sent]
        parts = tuple(len(blocks[k]) for k in steps)
        operands = [piece for k in steps for piece in blocks[k]]
        shape = (members, len(chosen), len(steps), capacity, width)
        slots = len(chosen) * members * capacity * len(steps)
        sent = call(
            functools.partial(slots_kernel, parts, chosen, local),
            jax.ShapeDtypeStruct(shape, bf16),
            (2 * slots * rows * width, 2 * slots * width),
            in_specs=[smem]
            + [whole(piece.shape) for piece in operands]
            + [pl.BlockSpec(memory_space=pl.ANY)] * len(awaited),
            out_specs=whole(shape),
        )(z_place, *operands, *awaited)
        got = lax.all_to_all(sent, "expert", 0, 0, axis_index_groups=planes, tiled=True)
        for at, j in enumerate(chosen):
            spec = pl.BlockSpec(
                (members, None) + shape[2:], lambda i, at=at: (0, at, 0, 0, 0)
            )
            arrivals[j].append((got, spec))

    new_momentum = None
    ahead, sent = [], []
    anywhere = pl.BlockSpec(memory_space=pl.ANY)
    lefts, raws = [], []
    for j in range(local):
        arrived = [part for part, _ in arrivals[j]]
        specs = [spec for _, spec in arrivals[j]]
        held_specs = [whole(ordered[j].shape)] * quarters
        weights = call(
            functools.partial(weigh_kernel, quarters),
            jax.ShapeDtypeStruct((rank, slot_count), f32),
            (6 * rank * slot_count * cols * quarters, 2 * slot_count * cols * quarters),
            in_specs=held_specs + [anywhere] * len(ahead),
            out_specs=whole((rank, slot_count)),
        )(*held[j], *ahead)
        part = call(
            functools.partial(project_kernel, len(CHUNKS)),
            jax.ShapeDtypeStruct((rank, width), f32),
            (6 * rank * slot_count * width, 2 * slot_count * width),
            in_specs=[whole((rank, slot_count)), of_expert(j, (rank, width))]
            + specs
            + [anywhere] * len(lefts),
            out_specs=whole((rank, width)),
        )(weights, old, *arrived, *lefts)
        moved = [part] + [lax.ppermute(part, "et", ring(quarters, d)) for d in range(1, quarters)]
        grads = call(
            functools.partial(gradient_kernel, len(CHUNKS), quarters),
            [jax.ShapeDtypeStruct((width, cols), bf16)] * quarters,
            (2 * slot_count * width * cols * quarters, 2 * 3 * slot_count * width),
            in_specs=specs + held_specs + [anywhere] * (1 + (len(sent) or 1)),
            out_specs=[whole((width, cols))] * quarters,
        )(*arrived, *held[j], part, *(last[2:3] if j == 0 else sent))
        grads = grads[:1] + passing(grads[1:], moved[1:])
        ahead = grads[:1]
        sent = [grads[0]] + [
            lax.ppermute(grads[d], "et", ring(quarters, quarters - d)) for d in range(1, quarters)
        ]
        left = call(
            factor_kernel,
            jax.ShapeDtypeStruct((quarters, rank, width), f32),
            (12 * rank * rank * depth, 8 * rank * depth),
            in_specs=[smem] + [whole((rank, width))] * quarters,
            out_specs=whole((quarters, rank, width)),
        )(scalar, *moved)
        raw = call(
            right_kernel,
            jax.ShapeDtypeStruct((rank, cols), f32),
            (12 * rank * depth * cols, 4 * depth * cols),
            in_specs=[smem, whole(left.shape), of_expert(j, (quarters, width, cols))]
            + [whole((width, cols))] * quarters,
            out_specs=whole((rank, cols)),
        )(scalar, left, blocks_of, *sent)
        earlier = [] if new_momentum is None else [new_momentum]
        new_momentum = call(
            update_kernel,
            jax.ShapeDtypeStruct(blocks_of.shape, bf16),
            (6 * rank * depth * cols, 6 * depth * cols),
            in_specs=[smem, whole(left.shape), whole(raw.shape), of_expert(j, (quarters, width, cols))]
            + [whole((width, cols))] * quarters
            + [pl.BlockSpec(memory_space=pl.ANY)] * len(earlier),
            out_specs=of_expert(j, (quarters, width, cols)),
            input_output_aliases={4 + quarters: 0} if earlier else {},
        )(scalar, left, raw, blocks_of, *sent, *earlier)
        lefts.append(left)
        raws.append(raw)
    raw = jnp.stack(raws)
    own = jnp.sum(raw * raw, axis=2, keepdims=True)
    sums = own
    for d in range(1, quarters):
        sums = sums + lax.ppermute(own, "et", ring(quarters, d))
    new_right = raw / jnp.sqrt(sums + epsilon)
    left_factor = jnp.stack(lefts).transpose(0, 2, 1, 3).reshape(local, rank, depth)
    return (new_momentum.reshape(momentum.shape), left_factor, new_right)


def solution(mesh):
    placed = (
        P("expert", "et"),
        P("expert", None),
        P("expert", None),
        P("expert", None, "et"),
        P("expert", None, "et"),
        P("expert", None, "et"),
    )
    return jax.shard_map(
        body,
        mesh=mesh,
        in_specs=placed,
        out_specs=(P("expert", None, "et"), P("expert", None, None), P("expert", None, "et")),
        check_vma=False,
    )
```

time: 523 us -> 196 us (0.37)
  blocking collectives: 356 us -> 0 us
  starting transfers between devices: 0.04 us -> 58 us
  Pallas kernels: 0 us -> 39.1 us
  matrix products: 36.9 us -> 0 us
  other arithmetic: 20.9 us -> 0.91 us
  local copies, waits for them, and re-layouts: 46.3 us -> 29.9 us
    all_to_all x1 -> x0, blocking collectives: 331 us -> none  [body(): lax.all_to_all(send_buffer, 'expert', split_axis=1, concat_axis=1, tiled=...]
    psum x1 -> x0, waiting for transfers between devices: 48.8 us -> none  [body(): projected = lax.psum(partial_value, 'et')]
    ppermute x0 -> x29, waiting for transfers between devices: none -> 43.6 us  [the longest x6 15.3 us: body(): lax.ppermute(grads[d], 'et', ring(quarters, quarters - d))]
    ppermute x0 -> x29, starting transfers between devices: none -> 43.4 us  [the longest x8 16 us: z_shift(): lax.ppermute(value, 'expert', [(device(x, z, c), device(x, z + step, c))...]
    pallas_call x0 -> x23, Pallas kernels: none -> 39.1 us  [the longest x2 8.8 us: body(): call(factor_kernel, jax.ShapeDtypeStruct((quarters, rank, width), f32), (...]
    dot_general x5 -> x0, matrix products: 34.8 us -> none  [the longest x1 9.41 us: body(): jnp.einsum('erd,erh->edh', left_factor, raw_right, precision=highest, pre...]
    unnamed x12 -> x100, local copies, waits for them, and re-layouts: 4.64 us -> 27 us
    scatter x1 -> x0, local copies, waits for them, and re-layouts: 19.6 us -> none  [body(): jnp.zeros((local_count * owners * capacity, width), jnp.bfloat16).at[target]]
  transfers between devices with their start and end apart: 1 -> 33, of which waited for: 1 -> 12; matrix products, arithmetic and copies ran while one was open for 0% -> 3% of each run, Pallas kernels for 0% -> 20%
where the time goes in v1:
time: 196 us; the launch traced here: 195 us
  starting transfers between devices  58 us (30%)
  waiting for transfers between devices  52.4 us (27%)
  Pallas kernels  39.1 us (20%)
  local copies, waits for them, and re-layouts  29.9 us (15%)
  between operations  14.4 us (7%)
    unnamed x100, local copies, waits for them, and re-layouts  27 us
    ppermute x8, starting transfers between devices, z_shift(): lax.ppermute(value, 'expert', [(device(x, z, c), device(x, z + step, c))...  16 us
    ppermute x6, waiting for transfers between devices, body(): lax.ppermute(grads[d], 'et', ring(quarters, quarters - d))  15.3 us
    all_to_all x3, starting transfers between devices, body(): lax.all_to_all(sent, 'expert', 0, 0, axis_index_groups=planes, tiled=True)  14.6 us
    ppermute x8, waiting for transfers between devices, z_shift(): lax.ppermute(value, 'expert', [(device(x, z, c), device(x, z + step, c))...  13.1 us
    ppermute x6, waiting for transfers between devices, body(): lax.ppermute(ordered[j], 'et', ring(quarters, d))  11.3 us
    ppermute x6, starting transfers between devices, body(): lax.ppermute(ordered[j], 'et', ring(quarters, d))  9.84 us
    pallas_call x2, Pallas kernels, body(): call(factor_kernel, jax.ShapeDtypeStruct((quarters, rank, width), f32), (...  8.8 us
  transfers between devices with their start and end apart: 33, of which 12 were waited for; matrix products, arithmetic and copies ran while one was open for 3% of the time, Pallas kernels for 20%

profile of v1, /device:TPU:2, one launch (start us, length us, event | category | flops | bytes accessed | tf_op | source)
XLA Modules:
  0.0 194.6 jit_solution(14571902877192775068)
XLA Ops:
  9.5 5.9 %collective-permute-start.4 = (bf16[144,896]{1,0:T(8,128)(2,1)S(1)}, bf16[144,896]{1,0:T(8,128)(2,1)S(1)}, u32[]{:S(2)}, u32[]{:S(2)}) collective-permute-start(bf16[144,896]{1,0:T(8,128)(2,1)S(1)} %shard_map.86.refs_0_), channel_id=1, source_target_pairs={{0,56},{4,60},{8,0},{12,4},{16,8},{20,12},{24,16},{28,20},{32,24},... | collective-permute-start | bytes 774152 | tf_op jit(solution)/shard_map/ppermute | solution.py:273
  18.5 3.0 %collective-permute-start.6 = (bf16[1120,256]{1,0:T(8,128)(2,1)}, bf16[1120,256]{1,0:T(8,128)(2,1)S(1)}, u32[]{:S(2)}, u32[]{:S(2)}) collective-permute-start(bf16[1120,256]{1,0:T(8,128)(2,1)} %get-tuple-element.26.refs_4_.refs_0_.refs_2_), channel_id=1, source_target_pairs={{0,3},{1,0},{2,1},{3,2},{4,7},{5,4},{6,5},{7,6},{8,11},{9,8},{10,9... | collective-permute-start | bytes 1720328 | tf_op jit(solution)/shard_map/ppermute | solution.py:305
  21.5 2.0 %copy-done = bf16[2,3584,256]{2,1,0:T(8,128)(2,1)S(1)} copy-done((bf16[2,3584,256]{2,1,0:T(8,128)(2,1)S(1)}, bf16[2,3584,256]{2,1,0:T(8,128)(2,1)}, u32[]{:S(2)}) %copy-start) | copy-done | bytes 3670040
  23.5 2.2 %shard_map.87.refs_3_ = f32[2,32,3584]{2,1,0:T(8,128)} custom-call(f32[2,32,256]{2,1,0:T(8,128)S(1)} %copy-done.44, bf16[2,3584,256]{2,1,0:T(8,128)(2,1)S(1)} %copy-done), custom_call_target="tpu_custom_call" | custom-call | flops 352321536 | bytes 3670016 | tf_op jit(solution)/shard_map/pallas_call | solution.py:308
  27.7 4.8 %all-to-all-start = ((bf16[8,2,3,16,896]{4,3,2,1,0:T(8,128)(2,1)}), bf16[8,2,3,16,896]{4,3,2,1,0:T(8,128)(2,1)S(1)}, u32[]{:S(2)}, u32[]{:S(2)}) async-start(bf16[8,2,3,16,896]{4,3,2,1,0:T(8,128)(2,1)} %shard_map.88.refs_6_), calls=%async_computation | async-start | bytes 2752512 | tf_op jit(solution)/shard_map/all_to_all | solution.py:347
  32.5 3.2 %collective-permute-start.2 = (bf16[1120,256]{1,0:T(8,128)(2,1)}, bf16[1120,256]{1,0:T(8,128)(2,1)}, u32[]{:S(2)}, u32[]{:S(2)}) collective-permute-start(bf16[1120,256]{1,0:T(8,128)(2,1)} %copy-done.20), channel_id=1, source_target_pairs={{0,3},{1,0},{2,1},{3,2},{4,7},{5,4},{6,5},{7,6},{8,11},{9,8},{10,9... | collective-permute-start | bytes 1720328 | tf_op jit(solution)/shard_map/ppermute | solution.py:305
  39.1 3.2 %collective-permute-start.8 = (bf16[144,896]{1,0:T(8,128)(2,1)}, bf16[144,896]{1,0:T(8,128)(2,1)S(1)}, u32[]{:S(2)}, u32[]{:S(2)}) collective-permute-start(bf16[144,896]{1,0:T(8,128)(2,1)} %get-tuple-element.28), channel_id=1, source_target_pairs={{0,56},{4,60},{8,0},{12,4},{16,8},{20,12},{24,16},{28,20},{32,24},... | collective-permute-start | bytes 774152 | tf_op jit(solution)/shard_map/ppermute | solution.py:273
  42.3 6.2 %collective-permute-done.7.refs_0_ = bf16[144,896]{1,0:T(8,128)(2,1)S(1)} collective-permute-done((bf16[144,896]{1,0:T(8,128)(2,1)}, bf16[144,896]{1,0:T(8,128)(2,1)S(1)}, u32[]{:S(2)}, u32[]{:S(2)}) %collective-permute-start.7) | collective-permute-done | bytes 258080 | tf_op jit(solution)/shard_map/ppermute | solution.py:273
  49.9 6.3 %collective-permute-done.2.refs_3_.refs_5_ = bf16[1120,256]{1,0:T(8,128)(2,1)} collective-permute-done((bf16[1120,256]{1,0:T(8,128)(2,1)}, bf16[1120,256]{1,0:T(8,128)(2,1)}, u32[]{:S(2)}, u32[]{:S(2)}) %collective-permute-start.2) | collective-permute-done | bytes 573472 | tf_op jit(solution)/shard_map/ppermute | solution.py:305
  56.2 3.2 %collective-permute-done.refs_2_.refs_1_.refs_3_ = bf16[1120,256]{1,0:T(8,128)(2,1)} collective-permute-done((bf16[1120,256]{1,0:T(8,128)(2,1)}, bf16[1120,256]{1,0:T(8,128)(2,1)}, u32[]{:S(2)}, u32[]{:S(2)}) %collective-permute-start) | collective-permute-done | bytes 573472 | tf_op jit(solution)/shard_map/ppermute | solution.py:305
  59.4 3.2 %collective-permute-start.10 = (bf16[144,896]{1,0:T(8,128)(2,1)}, bf16[144,896]{1,0:T(8,128)(2,1)S(1)}, u32[]{:S(2)}, u32[]{:S(2)}) collective-permute-start(bf16[144,896]{1,0:T(8,128)(2,1)} %get-tuple-element.30), channel_id=1, source_target_pairs={{0,56},{4,60},{8,0},{12,4},{16,8},{20,12},{24,16},{28,20},{32,24},... | collective-permute-start | bytes 774152 | tf_op jit(solution)/shard_map/ppermute | solution.py:273
  62.7 4.5 %collective-permute-done.9.refs_2_ = bf16[144,896]{1,0:T(8,128)(2,1)S(1)} collective-permute-done((bf16[144,896]{1,0:T(8,128)(2,1)}, bf16[144,896]{1,0:T(8,128)(2,1)S(1)}, u32[]{:S(2)}, u32[]{:S(2)}) %collective-permute-start.9) | collective-permute-done | bytes 258080 | tf_op jit(solution)/shard_map/ppermute | solution.py:273
  72.3 3.5 %collective-permute-start.13 = (bf16[64,896]{1,0:T(8,128)(2,1)S(1)}, bf16[64,896]{1,0:T(8,128)(2,1)S(1)}, u32[]{:S(2)}, u32[]{:S(2)}) collective-permute-start(bf16[64,896]{1,0:T(8,128)(2,1)S(1)} %slice.7), channel_id=1, source_target_pairs={{0,56},{4,60},{8,0},{12,4},{16,8},{20,12},{24,16},{28,20},{32,24},... | collective-permute-start | bytes 344072 | tf_op jit(solution)/shard_map/ppermute | solution.py:273
  75.8 2.4 %collective-permute-done.13.refs_5_ = bf16[64,896]{1,0:T(8,128)(2,1)S(1)} collective-permute-done((bf16[64,896]{1,0:T(8,128)(2,1)S(1)}, bf16[64,896]{1,0:T(8,128)(2,1)S(1)}, u32[]{:S(2)}, u32[]{:S(2)}) %collective-permute-start.13) | collective-permute-done | bytes 114720 | tf_op jit(solution)/shard_map/ppermute | solution.py:273
  78.1 2.1 %shard_map.92.refs_7_ = bf16[8,1,5,16,896]{4,3,2,1,0:T(8,128)(2,1)} custom-call(s32[1]{0:T(128)} %bitcast.1.place_ref, bf16[144,896]{1,0:T(8,128)(2,1)S(1)} %collective-permute-done.7.refs_0_, bf16[144,896]{1,0:T(8,128)(2,1)S(1)} %collective-permute-done.8.refs_1_, bf16[144,896]{1,0:T(8,128)(2,1)S(1)} %collective-permute-done.9.refs_2_, ...), custom_call_target="tpu_custom_call" | custom-call | flops 146800640 | bytes 1146880 | tf_op jit(solution)/shard_map/pallas_call | solution.py:338
  81.6 4.8 %all-to-all-start.1 = ((bf16[8,1,5,16,896]{4,3,2,1,0:T(8,128)(2,1)}), bf16[8,1,5,16,896]{4,3,2,1,0:T(8,128)(2,1)S(1)}, u32[]{:S(2)}, u32[]{:S(2)}) async-start(bf16[8,1,5,16,896]{4,3,2,1,0:T(8,128)(2,1)} %shard_map.92.refs_7_), calls=%async_computation.1 | async-start | bytes 2293760 | tf_op jit(solution)/shard_map/all_to_all | solution.py:347
  91.1 2.1 %shard_map.97 = bf16[8,1,5,16,896]{4,3,2,1,0:T(8,128)(2,1)} custom-call(s32[1]{0:T(128)} %bitcast.1.place_ref, bf16[144,896]{1,0:T(8,128)(2,1)S(1)} %collective-permute-done.7.refs_0_, bf16[144,896]{1,0:T(8,128)(2,1)S(1)} %collective-permute-done.8.refs_1_, bf16[144,896]{1,0:T(8,128)(2,1)S(1)} %collective-permute-done.9.refs_2_, ...), custom_call_target="tpu_custom_call" | custom-call | flops 146800640 | bytes 1146880 | tf_op jit(solution)/shard_map/pallas_call | solution.py:338
  93.2 8.7 %all-to-all-done.1.refs_1_ = bf16[8,1,5,16,896]{4,3,2,1,0:T(8,128)(2,1)S(1)} async-done(((bf16[8,1,5,16,896]{4,3,2,1,0:T(8,128)(2,1)}), bf16[8,1,5,16,896]{4,3,2,1,0:T(8,128)(2,1)S(1)}, u32[]{:S(2)}, u32[]{:S(2)}) %all-to-all-start.1) | async-done | bytes 1146912 | tf_op jit(solution)/shard_map/all_to_all | solution.py:347
  102.9 4.9 %all-to-all-start.2 = ((bf16[8,1,5,16,896]{4,3,2,1,0:T(8,128)(2,1)}), bf16[8,1,5,16,896]{4,3,2,1,0:T(8,128)(2,1)S(1)}, u32[]{:S(2)}, u32[]{:S(2)}) async-start(bf16[8,1,5,16,896]{4,3,2,1,0:T(8,128)(2,1)} %shard_map.97), calls=%async_computation.3 | async-start | bytes 2293760 | tf_op jit(solution)/shard_map/all_to_all | solution.py:347
  108.9 2.1 %shard_map.93.weights_ref = f32[32,1024]{1,0:T(8,128)S(1)} custom-call(bf16[1120,256]{1,0:T(8,128)(2,1)} %get-tuple-element.26.refs_4_.refs_0_.refs_2_, bf16[1120,256]{1,0:T(8,128)(2,1)S(1)} %copy-done.9, bf16[1120,256]{1,0:T(8,128)(2,1)} %collective-permute-done.11.refs_2_.refs_4_, bf16[1120,256]{1,0:T(8,128)(2,1)S(1)} %copy-done.6), custom_call_target="tpu_custom_call" | custom-call | flops 201326592 | bytes 2097152 | tf_op jit(solution)/shard_map/pallas_call | solution.py:362
  111.6 2.1 %collective-permute-start.15 = (f32[32,896]{1,0:T(8,128)S(1)}, f32[32,896]{1,0:T(8,128)S(1)}, u32[]{:S(2)}, u32[]{:S(2)}) collective-permute-start(f32[32,896]{1,0:T(8,128)S(1)} %shard_map.94.refs_6_.refs_0_), channel_id=1, source_target_pairs={{0,2},{1,3},{2,0},{3,1},{4,6},{5,7},{6,4},{7,5},{8,10},{9,11},{10,... | collective-permute-start | bytes 344072 | tf_op jit(solution)/shard_map/ppermute | solution.py:378
  115.0 3.8 %shard_map.95 = (bf16[896,256]{1,0:T(8,128)(2,1)S(1)}, bf16[896,256]{1,0:T(8,128)(2,1)S(1)}, bf16[896,256]{1,0:T(8,128)(2,1)S(1)}, bf16[896,256]{1,0:T(8,128)(2,1)S(1)}) custom-call(bf16[8,2,3,16,896]{4,3,2,1,0:T(8,128)(2,1)S(1)} %all-to-all-done.refs_0_, bf16[8,1,5,16,896]{4,3,2,1,0:T(8,128)(2,1)S(1)} %copy-done.4, ...), custom_call_target="tpu_custom_call" | custom-call | flops 1879048192 | bytes 5505024 | tf_op jit(solution)/shard_map/pallas_call | solution.py:379
  125.7 2.2 %shard_map.96.weights_ref = f32[32,1024]{1,0:T(8,128)S(1)} custom-call(bf16[1120,256]{1,0:T(8,128)(2,1)S(1)} %copy-done.21, bf16[1120,256]{1,0:T(8,128)(2,1)} %collective-permute-done.refs_2_.refs_1_.refs_3_, bf16[1120,256]{1,0:T(8,128)(2,1)} %collective-permute-done.1.refs_7_.refs_2_.refs_4_, bf16[1120,256]{1,0:T(8,128)(2,1)} %collective-permute-done.2.refs_3_.refs_5_, ...), custom_call_target="tpu_custom_call" | custom-call | flops 201326592 | bytes 2097152 | tf_op jit(solution)/shard_map/pallas_call | solution.py:362
  128.6 3.9 %shard_map.98.refs_2_.left_ref = f32[4,32,896]{2,1,0:T(8,128)S(1)} custom-call(s32[1]{0:T(128)} %bitcast.me_ref, f32[32,896]{1,0:T(8,128)S(1)} %shard_map.94.refs_6_.refs_0_, f32[32,896]{1,0:T(8,128)S(1)} %copy-done.32, f32[32,896]{1,0:T(8,128)S(1)} %copy-done.30, f32[32,896]{1,0:T(8,128)S(1)} %copy-done.28), custom_call_target="tpu_custom_call" | custom-call | flops 44040192 | bytes 917504 | tf_op jit(solution)/shard_map/pallas_call | solution.py:391
  134.8 2.7 %collective-permute-start.19 = (f32[32,896]{1,0:T(8,128)S(1)}, f32[32,896]{1,0:T(8,128)S(1)}, u32[]{:S(2)}, u32[]{:S(2)}) collective-permute-start(f32[32,896]{1,0:T(8,128)S(1)} %shard_map.99.refs_0_.refs_6_), channel_id=1, source_target_pairs={{0,3},{1,0},{2,1},{3,2},{4,7},{5,4},{6,5},{7,6},{8,11},{9,8},{10,9... | collective-permute-start | bytes 344072 | tf_op jit(solution)/shard_map/ppermute | solution.py:378
  139.3 7.7 %collective-permute-done.22.refs_10_.refs_3_ = bf16[896,256]{1,0:T(8,128)(2,1)} collective-permute-done((bf16[896,256]{1,0:T(8,128)(2,1)}, bf16[896,256]{1,0:T(8,128)(2,1)}, u32[]{:S(2)}, u32[]{:S(2)}) %collective-permute-start.22) | collective-permute-done | bytes 458784 | tf_op jit(solution)/shard_map/ppermute | solution.py:389
  147.0 4.0 %shard_map.102 = (bf16[896,256]{1,0:T(8,128)(2,1)S(1)}, bf16[896,256]{1,0:T(8,128)(2,1)S(1)}, bf16[896,256]{1,0:T(8,128)(2,1)S(1)}, bf16[896,256]{1,0:T(8,128)(2,1)S(1)}) custom-call(bf16[8,2,3,16,896]{4,3,2,1,0:T(8,128)(2,1)S(1)} %all-to-all-done.refs_0_, bf16[8,1,5,16,896]{4,3,2,1,0:T(8,128)(2,1)S(1)} %all-to-all-done.2.refs_1_, ...), custom_call_target="tpu_custom_call" | custom-call | flops 1879048192 | bytes 5505024 | tf_op jit(solution)/shard_map/pallas_call | solution.py:379
  157.7 2.0 %copy-done.1 = bf16[2,3584,256]{2,1,0:T(8,128)(2,1)S(1)} copy-done((bf16[2,3584,256]{2,1,0:T(8,128)(2,1)S(1)}, bf16[2,3584,256]{2,1,0:T(8,128)(2,1)}, u32[]{:S(2)}) %copy-start.1) | copy-done | bytes 3670040
  159.7 2.0 %shard_map.105.raw_ref = f32[32,256]{1,0:T(8,128)S(1)} custom-call(s32[1]{0:T(128)} %bitcast.me_ref, f32[4,32,896]{2,1,0:T(8,128)S(1)} %shard_map.98.refs_2_.left_ref, bf16[2,4,896,256]{3,2,1,0:T(8,128)(2,1)S(1)} %bitcast.19, bf16[896,256]{1,0:T(8,128)(2,1)S(1)} %get-tuple-element.33.refs_4_.refs_7_.refs_0_, ...), custom_call_target="tpu_custom_call" | custom-call | flops 352321536 | bytes 3670016 | tf_op jit(solution)/shard_map/pallas_call | solution.py:398
  161.8 3.3 %shard_map.106.refs_4_ = bf16[2,4,896,256]{3,2,1,0:T(8,128)(2,1)} custom-call(s32[1]{0:T(128)} %bitcast.me_ref, f32[4,32,896]{2,1,0:T(8,128)S(1)} %shard_map.98.refs_2_.left_ref, f32[32,256]{1,0:T(8,128)S(1)} %shard_map.105.raw_ref, bf16[2,4,896,256]{3,2,1,0:T(8,128)(2,1)S(1)} %bitcast.20, bf16[896,256]{1,0:T(8,128)(2,1)S(1)} %get-tuple-element.33.refs_4_.refs_7_.refs_0_, ...), custom_call_target="tpu_custom_call" | custom-call | flops 176160768 | bytes 5505024 | tf_op jit(solution)/shard_map/pallas_call | solution.py:407
  165.1 4.9 %shard_map.100.left_ref = f32[4,32,896]{2,1,0:T(8,128)S(1)} custom-call(s32[1]{0:T(128)} %bitcast.me_ref, f32[32,896]{1,0:T(8,128)S(1)} %copy-done.42, f32[32,896]{1,0:T(8,128)} %collective-permute-done.17.refs_1_.refs_3_, f32[32,896]{1,0:T(8,128)} %collective-permute-done.18.refs_2_.refs_4_, f32[32,896]{1,0:T(8,128)S(1)} %copy-done.26), custom_call_target="tpu_custom_call" | custom-call | flops 44040192 | bytes 917504 | tf_op jit(solution)/shard_map/pallas_call | solution.py:391
  171.3 7.4 %collective-permute-done.25.refs_3_ = bf16[896,256]{1,0:T(8,128)(2,1)S(1)} collective-permute-done((bf16[896,256]{1,0:T(8,128)(2,1)}, bf16[896,256]{1,0:T(8,128)(2,1)S(1)}, u32[]{:S(2)}, u32[]{:S(2)}) %collective-permute-start.25) | collective-permute-done | bytes 458784 | tf_op jit(solution)/shard_map/ppermute | solution.py:389
  (165 shorter events, 55.7 us)
Async XLA Ops:
  9.5 16.2 %collective-permute-start.4 = (bf16[144,896]{1,0:T(8,128)(2,1)S(1)}, bf16[144,896]{1,0:T(8,128)(2,1)S(1)}, u32[]{:S(2)}, u32[]{:S(2)}) collective-permute-start(bf16[144,896]{1,0:T(8,128)(2,1)S(1)} %shard_map.86.refs_0_), channel_id=1, source_target_pairs={{0,56},{4,60},{8,0},{12,4},{16,8},{20,12},{24,16},{28,20},{32,24},... | collective-permute-start | bytes 774152 | tf_op jit(solution)/shard_map/ppermute | solution.py:273
  15.5 10.2 %collective-permute-start.3 = (bf16[144,896]{1,0:T(8,128)(2,1)S(1)}, bf16[144,896]{1,0:T(8,128)(2,1)S(1)}, u32[]{:S(2)}, u32[]{:S(2)}) collective-permute-start(bf16[144,896]{1,0:T(8,128)(2,1)S(1)} %shard_map.86.refs_0_), channel_id=1, source_target_pairs={{0,8},{4,12},{8,16},{12,20},{16,24},{20,28},{24,32},{28,36},{32,40... | collective-permute-start | bytes 774152 | tf_op jit(solution)/shard_map/ppermute | solution.py:273
  18.5 19.0 %collective-permute-start.6 = (bf16[1120,256]{1,0:T(8,128)(2,1)}, bf16[1120,256]{1,0:T(8,128)(2,1)S(1)}, u32[]{:S(2)}, u32[]{:S(2)}) collective-permute-start(bf16[1120,256]{1,0:T(8,128)(2,1)} %get-tuple-element.26.refs_4_.refs_0_.refs_2_), channel_id=1, source_target_pairs={{0,3},{1,0},{2,1},{3,2},{4,7},{5,4},{6,5},{7,6},{8,11},{9,8},{10,9... | collective-permute-start | bytes 1720328 | tf_op jit(solution)/shard_map/ppermute | solution.py:305
  21.5 15.9 %collective-permute-start.5 = (bf16[1120,256]{1,0:T(8,128)(2,1)}, bf16[1120,256]{1,0:T(8,128)(2,1)S(1)}, u32[]{:S(2)}, u32[]{:S(2)}) collective-permute-start(bf16[1120,256]{1,0:T(8,128)(2,1)} %get-tuple-element.26.refs_4_.refs_0_.refs_2_), channel_id=1, source_target_pairs={{0,1},{1,2},{2,3},{3,0},{4,5},{5,6},{6,7},{7,4},{8,9},{9,10},{10,1... | collective-permute-start | bytes 1720328 | tf_op jit(solution)/shard_map/ppermute | solution.py:305
  27.7 53.9 %all-to-all-start = ((bf16[8,2,3,16,896]{4,3,2,1,0:T(8,128)(2,1)}), bf16[8,2,3,16,896]{4,3,2,1,0:T(8,128)(2,1)S(1)}, u32[]{:S(2)}, u32[]{:S(2)}) async-start(bf16[8,2,3,16,896]{4,3,2,1,0:T(8,128)(2,1)} %shard_map.88.refs_6_), calls=%async_computation | async-start | bytes 2752512 | tf_op jit(solution)/shard_map/all_to_all | solution.py:347
  32.5 55.8 %reduce-scatter.2.cloned.1.call-start = ((), (), s32[]{:S(2)}) async-start(), calls=%async_computation.4 | async-start | bytes 1146880 | tf_op jit(solution)/shard_map/reduce_scatter | solution.py:314
  32.5 23.7 %collective-permute-start.2 = (bf16[1120,256]{1,0:T(8,128)(2,1)}, bf16[1120,256]{1,0:T(8,128)(2,1)}, u32[]{:S(2)}, u32[]{:S(2)}) collective-permute-start(bf16[1120,256]{1,0:T(8,128)(2,1)} %copy-done.20), channel_id=1, source_target_pairs={{0,3},{1,0},{2,1},{3,2},{4,7},{5,4},{6,5},{7,6},{8,11},{9,8},{10,9... | collective-permute-start | bytes 1720328 | tf_op jit(solution)/shard_map/ppermute | solution.py:305
  35.8 23.7 %collective-permute-start = (bf16[1120,256]{1,0:T(8,128)(2,1)}, bf16[1120,256]{1,0:T(8,128)(2,1)}, u32[]{:S(2)}, u32[]{:S(2)}) collective-permute-start(bf16[1120,256]{1,0:T(8,128)(2,1)} %copy-done.20), channel_id=1, source_target_pairs={{0,1},{1,2},{2,3},{3,0},{4,5},{5,6},{6,7},{7,4},{8,9},{9,10},{10,1... | collective-permute-start | bytes 1720328 | tf_op jit(solution)/shard_map/ppermute | solution.py:305
  35.8 34.6 %collective-permute-start.11 = (bf16[1120,256]{1,0:T(8,128)(2,1)}, bf16[1120,256]{1,0:T(8,128)(2,1)}, u32[]{:S(2)}, u32[]{:S(2)}) collective-permute-start(bf16[1120,256]{1,0:T(8,128)(2,1)} %get-tuple-element.26.refs_4_.refs_0_.refs_2_), channel_id=1, source_target_pairs={{0,2},{1,3},{2,0},{3,1},{4,6},{5,7},{6,4},{7,5},{8,10},{9,11},{10,... | collective-permute-start | bytes 1720328 | tf_op jit(solution)/shard_map/ppermute | solution.py:305
  39.1 9.4 %collective-permute-start.7 = (bf16[144,896]{1,0:T(8,128)(2,1)}, bf16[144,896]{1,0:T(8,128)(2,1)S(1)}, u32[]{:S(2)}, u32[]{:S(2)}) collective-permute-start(bf16[144,896]{1,0:T(8,128)(2,1)} %get-tuple-element.27), channel_id=1, source_target_pairs={{0,8},{4,12},{8,16},{12,20},{16,24},{20,28},{24,32},{28,36},{32,40... | collective-permute-start | bytes 774152 | tf_op jit(solution)/shard_map/ppermute | solution.py:273
  39.1 10.1 %collective-permute-start.8 = (bf16[144,896]{1,0:T(8,128)(2,1)}, bf16[144,896]{1,0:T(8,128)(2,1)S(1)}, u32[]{:S(2)}, u32[]{:S(2)}) collective-permute-start(bf16[144,896]{1,0:T(8,128)(2,1)} %get-tuple-element.28), channel_id=1, source_target_pairs={{0,56},{4,60},{8,0},{12,4},{16,8},{20,12},{24,16},{28,20},{32,24},... | collective-permute-start | bytes 774152 | tf_op jit(solution)/shard_map/ppermute | solution.py:273
  59.4 7.8 %collective-permute-start.9 = (bf16[144,896]{1,0:T(8,128)(2,1)}, bf16[144,896]{1,0:T(8,128)(2,1)S(1)}, u32[]{:S(2)}, u32[]{:S(2)}) collective-permute-start(bf16[144,896]{1,0:T(8,128)(2,1)} %get-tuple-element.29), channel_id=1, source_target_pairs={{0,8},{4,12},{8,16},{12,20},{16,24},{20,28},{24,32},{28,36},{32,40... | collective-permute-start | bytes 774152 | tf_op jit(solution)/shard_map/ppermute | solution.py:273
  59.4 8.5 %collective-permute-start.10 = (bf16[144,896]{1,0:T(8,128)(2,1)}, bf16[144,896]{1,0:T(8,128)(2,1)S(1)}, u32[]{:S(2)}, u32[]{:S(2)}) collective-permute-start(bf16[144,896]{1,0:T(8,128)(2,1)} %get-tuple-element.30), channel_id=1, source_target_pairs={{0,56},{4,60},{8,0},{12,4},{16,8},{20,12},{24,16},{28,20},{32,24},... | collective-permute-start | bytes 774152 | tf_op jit(solution)/shard_map/ppermute | solution.py:273
  71.3 6.9 %collective-permute-start.12 = (bf16[80,896]{1,0:T(8,128)(2,1)S(1)}, bf16[80,896]{1,0:T(8,128)(2,1)S(1)}, u32[]{:S(2)}, u32[]{:S(2)}) collective-permute-start(bf16[80,896]{1,0:T(8,128)(2,1)S(1)} %slice.6), channel_id=1, source_target_pairs={{0,8},{4,12},{8,16},{12,20},{16,24},{20,28},{24,32},{28,36},{32,40... | collective-permute-start | bytes 430088 | tf_op jit(solution)/shard_map/ppermute | solution.py:273
  72.3 5.9 %collective-permute-start.13 = (bf16[64,896]{1,0:T(8,128)(2,1)S(1)}, bf16[64,896]{1,0:T(8,128)(2,1)S(1)}, u32[]{:S(2)}, u32[]{:S(2)}) collective-permute-start(bf16[64,896]{1,0:T(8,128)(2,1)S(1)} %slice.7), channel_id=1, source_target_pairs={{0,56},{4,60},{8,0},{12,4},{16,8},{20,12},{24,16},{28,20},{32,24},... | collective-permute-start | bytes 344072 | tf_op jit(solution)/shard_map/ppermute | solution.py:273
  81.6 20.4 %all-to-all-start.1 = ((bf16[8,1,5,16,896]{4,3,2,1,0:T(8,128)(2,1)}), bf16[8,1,5,16,896]{4,3,2,1,0:T(8,128)(2,1)S(1)}, u32[]{:S(2)}, u32[]{:S(2)}) async-start(bf16[8,1,5,16,896]{4,3,2,1,0:T(8,128)(2,1)} %shard_map.92.refs_7_), calls=%async_computation.1 | async-start | bytes 2293760 | tf_op jit(solution)/shard_map/all_to_all | solution.py:347
  86.4 28.6 %collective-permute-start.1 = (bf16[1120,256]{1,0:T(8,128)(2,1)}, bf16[1120,256]{1,0:T(8,128)(2,1)}, u32[]{:S(2)}, u32[]{:S(2)}) collective-permute-start(bf16[1120,256]{1,0:T(8,128)(2,1)} %copy-done.20), channel_id=1, source_target_pairs={{0,2},{1,3},{2,0},{3,1},{4,6},{5,7},{6,4},{7,5},{8,10},{9,11},{10,... | collective-permute-start | bytes 1720328 | tf_op jit(solution)/shard_map/ppermute | solution.py:305
  102.9 29.6 %all-to-all-start.2 = ((bf16[8,1,5,16,896]{4,3,2,1,0:T(8,128)(2,1)}), bf16[8,1,5,16,896]{4,3,2,1,0:T(8,128)(2,1)S(1)}, u32[]{:S(2)}, u32[]{:S(2)}) async-start(bf16[8,1,5,16,896]{4,3,2,1,0:T(8,128)(2,1)} %shard_map.97), calls=%async_computation.3 | async-start | bytes 2293760 | tf_op jit(solution)/shard_map/all_to_all | solution.py:347
  111.5 7.4 %collective-permute-start.16 = (f32[32,896]{1,0:T(8,128)S(1)}, f32[32,896]{1,0:T(8,128)S(1)}, u32[]{:S(2)}, u32[]{:S(2)}) collective-permute-start(f32[32,896]{1,0:T(8,128)S(1)} %shard_map.94.refs_6_.refs_0_), channel_id=1, source_target_pairs={{0,3},{1,0},{2,1},{3,2},{4,7},{5,4},{6,5},{7,6},{8,11},{9,8},{10,9... | collective-permute-start | bytes 344072 | tf_op jit(solution)/shard_map/ppermute | solution.py:378
  111.6 7.3 %collective-permute-start.15 = (f32[32,896]{1,0:T(8,128)S(1)}, f32[32,896]{1,0:T(8,128)S(1)}, u32[]{:S(2)}, u32[]{:S(2)}) collective-permute-start(f32[32,896]{1,0:T(8,128)S(1)} %shard_map.94.refs_6_.refs_0_), channel_id=1, source_target_pairs={{0,2},{1,3},{2,0},{3,1},{4,6},{5,7},{6,4},{7,5},{8,10},{9,11},{10,... | collective-permute-start | bytes 344072 | tf_op jit(solution)/shard_map/ppermute | solution.py:378
  113.7 7.2 %collective-permute-start.14 = (f32[32,896]{1,0:T(8,128)S(1)}, f32[32,896]{1,0:T(8,128)S(1)}, u32[]{:S(2)}, u32[]{:S(2)}) collective-permute-start(f32[32,896]{1,0:T(8,128)S(1)} %shard_map.94.refs_6_.refs_0_), channel_id=1, source_target_pairs={{0,1},{1,2},{2,3},{3,0},{4,5},{5,6},{6,7},{7,4},{8,9},{9,10},{10,1... | collective-permute-start | bytes 344072 | tf_op jit(solution)/shard_map/ppermute | solution.py:378
  121.5 16.9 %collective-permute-start.20 = (bf16[896,256]{1,0:T(8,128)(2,1)}, bf16[896,256]{1,0:T(8,128)(2,1)}, u32[]{:S(2)}, u32[]{:S(2)}) collective-permute-start(bf16[896,256]{1,0:T(8,128)(2,1)} %get-tuple-element.37), channel_id=1, source_target_pairs={{0,3},{1,0},{2,1},{3,2},{4,7},{5,4},{6,5},{7,6},{8,11},{9,8},{10,9... | collective-permute-start | bytes 1376264 | tf_op jit(solution)/shard_map/ppermute | solution.py:389
  122.6 16.7 %collective-permute-start.21 = (bf16[896,256]{1,0:T(8,128)(2,1)}, bf16[896,256]{1,0:T(8,128)(2,1)}, u32[]{:S(2)}, u32[]{:S(2)}) collective-permute-start(bf16[896,256]{1,0:T(8,128)(2,1)} %get-tuple-element.38), channel_id=1, source_target_pairs={{0,2},{1,3},{2,0},{3,1},{4,6},{5,7},{6,4},{7,5},{8,10},{9,11},{10,... | collective-permute-start | bytes 1376264 | tf_op jit(solution)/shard_map/ppermute | solution.py:389
  124.1 23.0 %collective-permute-start.22 = (bf16[896,256]{1,0:T(8,128)(2,1)}, bf16[896,256]{1,0:T(8,128)(2,1)}, u32[]{:S(2)}, u32[]{:S(2)}) collective-permute-start(bf16[896,256]{1,0:T(8,128)(2,1)} %get-tuple-element.39), channel_id=1, source_target_pairs={{0,1},{1,2},{2,3},{3,0},{4,5},{5,6},{6,7},{7,4},{8,9},{9,10},{10,1... | collective-permute-start | bytes 1376264 | tf_op jit(solution)/shard_map/ppermute | solution.py:389
  134.8 19.3 %collective-permute-start.19 = (f32[32,896]{1,0:T(8,128)S(1)}, f32[32,896]{1,0:T(8,128)S(1)}, u32[]{:S(2)}, u32[]{:S(2)}) collective-permute-start(f32[32,896]{1,0:T(8,128)S(1)} %shard_map.99.refs_0_.refs_6_), channel_id=1, source_target_pairs={{0,3},{1,0},{2,1},{3,2},{4,7},{5,4},{6,5},{7,6},{8,11},{9,8},{10,9... | collective-permute-start | bytes 344072 | tf_op jit(solution)/shard_map/ppermute | solution.py:378
  137.6 16.6 %collective-permute-start.18 = (f32[32,896]{1,0:T(8,128)S(1)}, f32[32,896]{1,0:T(8,128)}, u32[]{:S(2)}, u32[]{:S(2)}) collective-permute-start(f32[32,896]{1,0:T(8,128)S(1)} %shard_map.99.refs_0_.refs_6_), channel_id=1, source_target_pairs={{0,2},{1,3},{2,0},{3,1},{4,6},{5,7},{6,4},{7,5},{8,10},{9,11},{10,... | collective-permute-start | bytes 344072 | tf_op jit(solution)/shard_map/ppermute | solution.py:378
  138.4 15.7 %collective-permute-start.17 = (f32[32,896]{1,0:T(8,128)S(1)}, f32[32,896]{1,0:T(8,128)}, u32[]{:S(2)}, u32[]{:S(2)}) collective-permute-start(f32[32,896]{1,0:T(8,128)S(1)} %shard_map.99.refs_0_.refs_6_), channel_id=1, source_target_pairs={{0,1},{1,2},{2,3},{3,0},{4,5},{5,6},{6,7},{7,4},{8,9},{9,10},{10,1... | collective-permute-start | bytes 344072 | tf_op jit(solution)/shard_map/ppermute | solution.py:378
  154.8 16.3 %collective-permute-start.23 = (bf16[896,256]{1,0:T(8,128)(2,1)}, bf16[896,256]{1,0:T(8,128)(2,1)S(1)}, u32[]{:S(2)}, u32[]{:S(2)}) collective-permute-start(bf16[896,256]{1,0:T(8,128)(2,1)} %get-tuple-element.44), channel_id=1, source_target_pairs={{0,3},{1,0},{2,1},{3,2},{4,7},{5,4},{6,5},{7,6},{8,11},{9,8},{10,9... | collective-permute-start | bytes 1376264 | tf_op jit(solution)/shard_map/ppermute | solution.py:389
  156.1 15.2 %collective-permute-start.24 = (bf16[896,256]{1,0:T(8,128)(2,1)}, bf16[896,256]{1,0:T(8,128)(2,1)S(1)}, u32[]{:S(2)}, u32[]{:S(2)}) collective-permute-start(bf16[896,256]{1,0:T(8,128)(2,1)} %get-tuple-element.45), channel_id=1, source_target_pairs={{0,2},{1,3},{2,0},{3,1},{4,6},{5,7},{6,4},{7,5},{8,10},{9,11},{10,... | collective-permute-start | bytes 1376264 | tf_op jit(solution)/shard_map/ppermute | solution.py:389
  157.5 21.2 %collective-permute-start.25 = (bf16[896,256]{1,0:T(8,128)(2,1)}, bf16[896,256]{1,0:T(8,128)(2,1)S(1)}, u32[]{:S(2)}, u32[]{:S(2)}) collective-permute-start(bf16[896,256]{1,0:T(8,128)(2,1)} %get-tuple-element.46), channel_id=1, source_target_pairs={{0,1},{1,2},{2,3},{3,0},{4,5},{5,6},{6,7},{7,4},{8,9},{9,10},{10,1... | collective-permute-start | bytes 1376264 | tf_op jit(solution)/shard_map/ppermute | solution.py:389
  179.5 5.5 %collective-permute-start.27 = (f32[2,32,1]{1,0,2:T(2,128)S(1)}, f32[2,32,1]{1,0,2:T(2,128)S(1)}, u32[]{:S(2)}, u32[]{:S(2)}) collective-permute-start(f32[2,32,1]{1,0,2:T(2,128)S(1)} %bitcast.34), channel_id=1, source_target_pairs={{0,2},{1,3},{2,0},{3,1},{4,6},{5,7},{6,4},{7,5},{8,10},{9,11},{10,... | collective-permute-start | bytes 776 | tf_op jit(solution)/shard_map/ppermute | solution.py:423
  182.3 4.8 %collective-permute-start.26 = (f32[2,32,1]{1,0,2:T(2,128)S(1)}, f32[2,32,1]{1,0,2:T(2,128)S(1)}, u32[]{:S(2)}, u32[]{:S(2)}) collective-permute-start(f32[2,32,1]{1,0,2:T(2,128)S(1)} %bitcast.36), channel_id=1, source_target_pairs={{0,1},{1,2},{2,3},{3,0},{4,5},{5,6},{6,7},{7,4},{8,9},{9,10},{10,1... | collective-permute-start | bytes 776 | tf_op jit(solution)/shard_map/ppermute | solution.py:423
  (49 other events, 148.9 us)
Sparse Core Ops, SparseCore 0:
  36.5 35.9 reduce-scatter.1

commit v2 on v1

--- a/solution.py
+++ b/solution.py
@@ -316,7 +316,7 @@
     blocks = {0: [packed]}
     up = down = packed
     first, last = held
-    gates_at = {1: first[1::2], 2: last[1::2], 3: first[2:3]}
+    gates_at = {1: first[1::2], 3: last[1::2]}
     for k in range(1, along_z // 2):
         up, down = z_shift(up, 1), z_shift(down, -1)
         blocks[k], blocks[-k] = [up], [down]
@@ -325,8 +325,17 @@
     half = 80
     blocks[along_z // 2] = [z_shift(up[:half], 1), z_shift(down[half:], -1)]
 
+    weights = [
+        call(
+            functools.partial(weigh_kernel, quarters),
+            jax.ShapeDtypeStruct((rank, slot_count), f32),
+            (6 * rank * slot_count * cols * quarters, 2 * slot_count * cols * quarters),
+        )(*held[j])
+        for j in range(local)
+    ]
     plan = [(CHUNKS[0], tuple(range(local)), [partial])]
-    plan += [(CHUNKS[1], (0,), []), (CHUNKS[1], (1,), [old])]
+    plan += [(CHUNKS[1], (0,), first[2:3])]
+    plan += [(CHUNKS[1], (1,), [old, weights[0]])]
     arrivals = [[] for _ in range(local)]
     sent = ordered[0]
     for steps, chosen, awaited in plan:
@@ -352,39 +361,32 @@
             arrivals[j].append((got, spec))
 
     new_momentum = None
-    ahead, sent = [], []
+    sent, ahead = [], []
     anywhere = pl.BlockSpec(memory_space=pl.ANY)
     lefts, raws = [], []
     for j in range(local):
         arrived = [part for part, _ in arrivals[j]]
         specs = [spec for _, spec in arrivals[j]]
         held_specs = [whole(ordered[j].shape)] * quarters
-        weights = call(
-            functools.partial(weigh_kernel, quarters),
-            jax.ShapeDtypeStruct((rank, slot_count), f32),
-            (6 * rank * slot_count * cols * quarters, 2 * slot_count * cols * quarters),
-            in_specs=held_specs + [anywhere] * len(ahead),
-            out_specs=whole((rank, slot_count)),
-        )(*held[j], *ahead)
         part = call(
             functools.partial(project_kernel, len(CHUNKS)),
             jax.ShapeDtypeStruct((rank, width), f32),
             (6 * rank * slot_count * width, 2 * slot_count * width),
             in_specs=[whole((rank, slot_count)), of_expert(j, (rank, width))]
             + specs
-            + [anywhere] * len(lefts),
+            + [anywhere] * len(ahead),
             out_specs=whole((rank, width)),
-        )(weights, old, *arrived, *lefts)
+        )(weights[j], old, *arrived, *ahead)
         moved = [part] + [lax.ppermute(part, "et", ring(quarters, d)) for d in range(1, quarters)]
         grads = call(
             functools.partial(gradient_kernel, len(CHUNKS), quarters),
             [jax.ShapeDtypeStruct((width, cols), bf16)] * quarters,
             (2 * slot_count * width * cols * quarters, 2 * 3 * slot_count * width),
-            in_specs=specs + held_specs + [anywhere] * (1 + (len(sent) or 1)),
+            in_specs=specs + held_specs + [anywhere] * (2 if j == 0 else 1),
             out_specs=[whole((width, cols))] * quarters,
-        )(*arrived, *held[j], part, *(last[2:3] if j == 0 else sent))
-        grads = grads[:1] + passing(grads[1:], moved[1:])
-        ahead = grads[:1]
+        )(*arrived, *held[j], part, *(last[2:3] if j == 0 else []))
+        grads = grads[:1] + passing(grads[1:], moved[1:] + sent[1:])
+        ahead = moved[1:]
         sent = [grads[0]] + [
             lax.ppermute(grads[d], "et", ring(quarters, quarters - d)) for d in range(1, quarters)
         ]

time: 196 us -> 186 us (0.949)
  waiting for transfers between devices: 52.4 us -> 36.3 us
  local copies, waits for them, and re-layouts: 29.9 us -> 36.8 us
  Pallas kernels: 39.1 us -> 36.7 us
    ppermute x6, waiting for transfers between devices: 15.3 us -> 6.69 us  [body(): lax.ppermute(grads[d], 'et', ring(quarters, quarters - d))]
    unnamed x100 -> x132, local copies, waits for them, and re-layouts: 27 us -> 33.9 us
    all_to_all x3, waiting for transfers between devices: 8.75 us -> 5.49 us  [body(): lax.all_to_all(sent, 'expert', 0, 0, axis_index_groups=planes, tiled=True)]
    ppermute x6, starting transfers between devices: 6.06 us -> 9.08 us  [body(): lax.ppermute(grads[d], 'et', ring(quarters, quarters - d))]
    ppermute x6, waiting for transfers between devices: 11.3 us -> 8.38 us  [body(): lax.ppermute(ordered[j], 'et', ring(quarters, d))]
    ppermute x8, waiting for transfers between devices: 13.1 us -> 10.3 us  [z_shift(): lax.ppermute(value, 'expert', [(device(x, z, c), device(x, z + step, c))...]
  transfers between devices with their start and end apart: 33 -> 33, of which waited for: 12 -> 11; matrix products, arithmetic and copies ran while one was open for 3% -> 2% of each run, Pallas kernels for 20% -> 19%
where the time goes in v2:
time: 186 us; the launch traced here: 185 us
  starting transfers between devices  59.7 us (32%)
  local copies, waits for them, and re-layouts  36.8 us (20%)
  Pallas kernels  36.7 us (20%)
  waiting for transfers between devices  36.3 us (20%)
  between operations  14.5 us (8%)
    unnamed x132, local copies, waits for them, and re-layouts  33.9 us
    ppermute x8, starting transfers between devices, z_shift(): lax.ppermute(value, 'expert', [(device(x, z, c), device(x, z + step, c))...  16 us
    all_to_all x3, starting transfers between devices, body(): lax.all_to_all(sent, 'expert', 0, 0, axis_index_groups=planes, tiled=True)  14.6 us
    ppermute x8, waiting for transfers between devices, z_shift(): lax.ppermute(value, 'expert', [(device(x, z, c), device(x, z + step, c))...  10.3 us
    ppermute x6, starting transfers between devices, body(): lax.ppermute(ordered[j], 'et', ring(quarters, d))  9.82 us
    ppermute x6, starting transfers between devices, body(): lax.ppermute(grads[d], 'et', ring(quarters, quarters - d))  9.08 us
    ppermute x6, waiting for transfers between devices, body(): lax.ppermute(ordered[j], 'et', ring(quarters, d))  8.38 us
    pallas_call x2, Pallas kernels, body(): call(functools.partial(gradient_kernel, len(CHUNKS), quarters), [jax.Shap...  7.93 us
  transfers between devices with their start and end apart: 33, of which 11 were waited for; matrix products, arithmetic and copies ran while one was open for 2% of the time, Pallas kernels for 19%

profile of v2, /device:TPU:2, one launch (start us, length us, event | category | flops | bytes accessed | tf_op | source)
XLA Modules:
  0.0 184.8 jit_solution(6787112095819211684)
XLA Ops:
  9.5 5.9 %collective-permute-start.4 = (bf16[144,896]{1,0:T(8,128)(2,1)S(1)}, bf16[144,896]{1,0:T(8,128)(2,1)S(1)}, u32[]{:S(2)}, u32[]{:S(2)}) collective-permute-start(bf16[144,896]{1,0:T(8,128)(2,1)S(1)} %shard_map.88.refs_0_), channel_id=1, source_target_pairs={{0,56},{4,60},{8,0},{12,4},{16,8},{20,12},{24,16},{28,20},{32,24},... | collective-permute-start | bytes 774152 | tf_op jit(solution)/shard_map/ppermute | solution.py:273
  18.6 3.0 %collective-permute-start.6 = (bf16[1120,256]{1,0:T(8,128)(2,1)}, bf16[1120,256]{1,0:T(8,128)(2,1)S(1)}, u32[]{:S(2)}, u32[]{:S(2)}) collective-permute-start(bf16[1120,256]{1,0:T(8,128)(2,1)} %get-tuple-element.24.refs_4_.refs_0_.refs_2_), channel_id=1, source_target_pairs={{0,3},{1,0},{2,1},{3,2},{4,7},{5,4},{6,5},{7,6},{8,11},{9,8},{10,9... | collective-permute-start | bytes 1720328 | tf_op jit(solution)/shard_map/ppermute | solution.py:305
  21.7 2.0 %copy-done = bf16[2,3584,256]{2,1,0:T(8,128)(2,1)S(1)} copy-done((bf16[2,3584,256]{2,1,0:T(8,128)(2,1)S(1)}, bf16[2,3584,256]{2,1,0:T(8,128)(2,1)}, u32[]{:S(2)}) %copy-start) | copy-done | bytes 3670040
  23.7 2.2 %shard_map.87.refs_3_ = f32[2,32,3584]{2,1,0:T(8,128)} custom-call(f32[2,32,256]{2,1,0:T(8,128)S(1)} %copy-done.61, bf16[2,3584,256]{2,1,0:T(8,128)(2,1)S(1)} %copy-done), custom_call_target="tpu_custom_call" | custom-call | flops 352321536 | bytes 3670016 | tf_op jit(solution)/shard_map/pallas_call | solution.py:308
  25.9 2.0 %shard_map.89.refs_7_ = bf16[8,2,3,16,896]{4,3,2,1,0:T(8,128)(2,1)} custom-call(s32[1]{0:T(128)} %bitcast.1.place_ref, bf16[144,896]{1,0:T(8,128)(2,1)S(1)} %shard_map.88.refs_0_, bf16[144,896]{1,0:T(8,128)(2,1)S(1)} %collective-permute-done.3.refs_1_.refs_0_, bf16[144,896]{1,0:T(8,128)(2,1)S(1)} %collective-permute-done.4.refs_2_.refs_1_, ...), custom_call_target="tpu_custom_call" | custom-call | flops 176160768 | bytes 1376256 | tf_op jit(solution)/shard_map/pallas_call | solution.py:347
  27.9 4.8 %all-to-all-start = ((bf16[8,2,3,16,896]{4,3,2,1,0:T(8,128)(2,1)}), bf16[8,2,3,16,896]{4,3,2,1,0:T(8,128)(2,1)S(1)}, u32[]{:S(2)}, u32[]{:S(2)}) async-start(bf16[8,2,3,16,896]{4,3,2,1,0:T(8,128)(2,1)} %shard_map.89.refs_7_), calls=%async_computation.1 | async-start | bytes 2752512 | tf_op jit(solution)/shard_map/all_to_all | solution.py:356
  33.4 3.3 %collective-permute-start.2 = (bf16[1120,256]{1,0:T(8,128)(2,1)}, bf16[1120,256]{1,0:T(8,128)(2,1)S(1)}, u32[]{:S(2)}, u32[]{:S(2)}) collective-permute-start(bf16[1120,256]{1,0:T(8,128)(2,1)} %get-tuple-element.23.refs_0_.refs_2_), channel_id=1, source_target_pairs={{0,3},{1,0},{2,1},{3,2},{4,7},{5,4},{6,5},{7,6},{8,11},{9,8},{10,9... | collective-permute-start | bytes 1720328 | tf_op jit(solution)/shard_map/ppermute | solution.py:305
  37.5 3.2 %collective-permute-start.8 = (bf16[144,896]{1,0:T(8,128)(2,1)}, bf16[144,896]{1,0:T(8,128)(2,1)S(1)}, u32[]{:S(2)}, u32[]{:S(2)}) collective-permute-start(bf16[144,896]{1,0:T(8,128)(2,1)} %get-tuple-element.26), channel_id=1, source_target_pairs={{0,56},{4,60},{8,0},{12,4},{16,8},{20,12},{24,16},{28,20},{32,24},... | collective-permute-start | bytes 774152 | tf_op jit(solution)/shard_map/ppermute | solution.py:273
  42.3 4.9 %collective-permute-done.7.refs_0_ = bf16[144,896]{1,0:T(8,128)(2,1)S(1)} collective-permute-done((bf16[144,896]{1,0:T(8,128)(2,1)}, bf16[144,896]{1,0:T(8,128)(2,1)S(1)}, u32[]{:S(2)}, u32[]{:S(2)}) %collective-permute-start.7) | collective-permute-done | bytes 258080 | tf_op jit(solution)/shard_map/ppermute | solution.py:273
  47.2 3.2 %collective-permute-start.10 = (bf16[144,896]{1,0:T(8,128)(2,1)S(1)}, bf16[144,896]{1,0:T(8,128)(2,1)S(1)}, u32[]{:S(2)}, u32[]{:S(2)}) collective-permute-start(bf16[144,896]{1,0:T(8,128)(2,1)S(1)} %collective-permute-done.8.refs_1_), channel_id=1, source_target_pairs={{0,56},{4,60},{8,0},{12,4},{16,8},{20,12},{24,16},{28,20},{32,24},... | collective-permute-start | bytes 774152 | tf_op jit(solution)/shard_map/ppermute | solution.py:273
  50.5 5.4 %collective-permute-done.9.refs_2_ = bf16[144,896]{1,0:T(8,128)(2,1)S(1)} collective-permute-done((bf16[144,896]{1,0:T(8,128)(2,1)S(1)}, bf16[144,896]{1,0:T(8,128)(2,1)S(1)}, u32[]{:S(2)}, u32[]{:S(2)}) %collective-permute-start.9) | collective-permute-done | bytes 258080 | tf_op jit(solution)/shard_map/ppermute | solution.py:273
  57.3 3.5 %collective-permute-done.refs_1_.refs_2_.refs_3_ = bf16[1120,256]{1,0:T(8,128)(2,1)S(1)} collective-permute-done((bf16[1120,256]{1,0:T(8,128)(2,1)}, bf16[1120,256]{1,0:T(8,128)(2,1)S(1)}, u32[]{:S(2)}, u32[]{:S(2)}) %collective-permute-start) | collective-permute-done | bytes 573472 | tf_op jit(solution)/shard_map/ppermute | solution.py:305
  63.6 3.5 %collective-permute-start.12 = (bf16[64,896]{1,0:T(8,128)(2,1)S(1)}, bf16[64,896]{1,0:T(8,128)(2,1)S(1)}, u32[]{:S(2)}, u32[]{:S(2)}) collective-permute-start(bf16[64,896]{1,0:T(8,128)(2,1)S(1)} %slice.7), channel_id=1, source_target_pairs={{0,56},{4,60},{8,0},{12,4},{16,8},{20,12},{24,16},{28,20},{32,24},... | collective-permute-start | bytes 344072 | tf_op jit(solution)/shard_map/ppermute | solution.py:273
  67.1 4.3 %collective-permute-done.13.refs_2_.refs_6_.refs_4_ = bf16[1120,256]{1,0:T(8,128)(2,1)} collective-permute-done((bf16[1120,256]{1,0:T(8,128)(2,1)}, bf16[1120,256]{1,0:T(8,128)(2,1)}, u32[]{:S(2)}, u32[]{:S(2)}) %collective-permute-start.13) | collective-permute-done | bytes 573472 | tf_op jit(solution)/shard_map/ppermute | solution.py:305
  72.3 2.1 %shard_map.93.refs_8_ = bf16[8,1,5,16,896]{4,3,2,1,0:T(8,128)(2,1)} custom-call(s32[1]{0:T(128)} %bitcast.1.place_ref, bf16[144,896]{1,0:T(8,128)(2,1)S(1)} %collective-permute-done.7.refs_0_, bf16[144,896]{1,0:T(8,128)(2,1)S(1)} %copy-done.28, bf16[144,896]{1,0:T(8,128)(2,1)S(1)} %collective-permute-done.9.refs_2_, ...), custom_call_target="tpu_custom_call" | custom-call | flops 146800640 | bytes 1146880 | tf_op jit(solution)/shard_map/pallas_call | solution.py:347
  75.0 4.8 %all-to-all-start.2 = ((bf16[8,1,5,16,896]{4,3,2,1,0:T(8,128)(2,1)}), bf16[8,1,5,16,896]{4,3,2,1,0:T(8,128)(2,1)S(1)}, u32[]{:S(2)}, u32[]{:S(2)}) async-start(bf16[8,1,5,16,896]{4,3,2,1,0:T(8,128)(2,1)} %shard_map.93.refs_8_), calls=%async_computation.3 | async-start | bytes 2293760 | tf_op jit(solution)/shard_map/all_to_all | solution.py:356
  82.9 2.1 %shard_map.92.refs_7_.weights_ref = f32[32,1024]{1,0:T(8,128)S(1)} custom-call(bf16[1120,256]{1,0:T(8,128)(2,1)} %get-tuple-element.24.refs_4_.refs_0_.refs_2_, bf16[1120,256]{1,0:T(8,128)(2,1)} %collective-permute-done.5.refs_2_.refs_1_.refs_3_, bf16[1120,256]{1,0:T(8,128)(2,1)} %collective-permute-done.13.refs_2_.refs_6_.refs_4_, ...), custom_call_target="tpu_custom_call" | custom-call | flops 201326592 | bytes 2097152 | tf_op jit(solution)/shard_map/pallas_call | solution.py:329
  89.9 5.5 %all-to-all-done.2.refs_1_ = bf16[8,1,5,16,896]{4,3,2,1,0:T(8,128)(2,1)S(1)} async-done(((bf16[8,1,5,16,896]{4,3,2,1,0:T(8,128)(2,1)}), bf16[8,1,5,16,896]{4,3,2,1,0:T(8,128)(2,1)S(1)}, u32[]{:S(2)}, u32[]{:S(2)}) %all-to-all-start.2) | async-done | bytes 1146912 | tf_op jit(solution)/shard_map/all_to_all | solution.py:356
  96.4 4.9 %all-to-all-start.1 = ((bf16[8,1,5,16,896]{4,3,2,1,0:T(8,128)(2,1)}), bf16[8,1,5,16,896]{4,3,2,1,0:T(8,128)(2,1)S(1)}, u32[]{:S(2)}, u32[]{:S(2)}) async-start(bf16[8,1,5,16,896]{4,3,2,1,0:T(8,128)(2,1)} %copy-done.3), calls=%async_computation.2 | async-start | bytes 2293760 | tf_op jit(solution)/shard_map/all_to_all | solution.py:356
  103.2 2.0 %collective-permute-start.15 = (f32[32,896]{1,0:T(8,128)S(1)}, f32[32,896]{1,0:T(8,128)S(1)}, u32[]{:S(2)}, u32[]{:S(2)}) collective-permute-start(f32[32,896]{1,0:T(8,128)S(1)} %shard_map.95.refs_6_.refs_0_), channel_id=1, source_target_pairs={{0,2},{1,3},{2,0},{3,1},{4,6},{5,7},{6,4},{7,5},{8,10},{9,11},{10,... | collective-permute-start | bytes 344072 | tf_op jit(solution)/shard_map/ppermute | solution.py:380
  106.5 4.0 %shard_map.99 = (bf16[896,256]{1,0:T(8,128)(2,1)S(1)}, bf16[896,256]{1,0:T(8,128)(2,1)S(1)}, bf16[896,256]{1,0:T(8,128)(2,1)S(1)}, bf16[896,256]{1,0:T(8,128)(2,1)S(1)}) custom-call(bf16[8,2,3,16,896]{4,3,2,1,0:T(8,128)(2,1)S(1)} %all-to-all-done.refs_0_, bf16[8,1,5,16,896]{4,3,2,1,0:T(8,128)(2,1)S(1)} %copy-done.5, ...), custom_call_target="tpu_custom_call" | custom-call | flops 1879048192 | bytes 5505024 | tf_op jit(solution)/shard_map/pallas_call | solution.py:381
  120.7 2.0 %shard_map.86.weights_ref = f32[32,1024]{1,0:T(8,128)S(1)} custom-call(bf16[1120,256]{1,0:T(8,128)(2,1)} %get-tuple-element.23.refs_0_.refs_2_, bf16[1120,256]{1,0:T(8,128)(2,1)S(1)} %copy-done.14, bf16[1120,256]{1,0:T(8,128)(2,1)} %collective-permute-done.1.refs_2_.refs_4_.refs_7_, bf16[1120,256]{1,0:T(8,128)(2,1)S(1)} %copy-done.11), custom_call_target="tpu_custom_call" | custom-call | flops 201326592 | bytes 2097152 | tf_op jit(solution)/shard_map/pallas_call | solution.py:329
  130.9 4.7 %collective-permute-done.20.refs_6_.refs_1_ = bf16[896,256]{1,0:T(8,128)(2,1)S(1)} collective-permute-done((bf16[896,256]{1,0:T(8,128)(2,1)}, bf16[896,256]{1,0:T(8,128)(2,1)S(1)}, u32[]{:S(2)}, u32[]{:S(2)}) %collective-permute-start.20) | collective-permute-done | bytes 458784 | tf_op jit(solution)/shard_map/ppermute | solution.py:391
  135.6 4.0 %shard_map.98 = (bf16[896,256]{1,0:T(8,128)(2,1)S(1)}, bf16[896,256]{1,0:T(8,128)(2,1)S(1)}, bf16[896,256]{1,0:T(8,128)(2,1)S(1)}, bf16[896,256]{1,0:T(8,128)(2,1)S(1)}) custom-call(bf16[8,2,3,16,896]{4,3,2,1,0:T(8,128)(2,1)S(1)} %all-to-all-done.refs_0_, bf16[8,1,5,16,896]{4,3,2,1,0:T(8,128)(2,1)S(1)} %all-to-all-done.1.refs_1_, ...), custom_call_target="tpu_custom_call" | custom-call | flops 1879048192 | bytes 5505024 | tf_op jit(solution)/shard_map/pallas_call | solution.py:381
  145.2 2.1 %collective-permute-start.23 = (bf16[896,256]{1,0:T(8,128)(2,1)}, bf16[896,256]{1,0:T(8,128)(2,1)S(1)}, u32[]{:S(2)}, u32[]{:S(2)}) collective-permute-start(bf16[896,256]{1,0:T(8,128)(2,1)} %get-tuple-element.39), channel_id=1, source_target_pairs={{0,3},{1,0},{2,1},{3,2},{4,7},{5,4},{6,5},{7,6},{8,11},{9,8},{10,9... | collective-permute-start | bytes 1376264 | tf_op jit(solution)/shard_map/ppermute | solution.py:391
  150.1 3.9 %shard_map.103.left_ref = f32[4,32,896]{2,1,0:T(8,128)S(1)} custom-call(s32[1]{0:T(128)} %bitcast.me_ref, f32[32,896]{1,0:T(8,128)S(1)} %copy-done.45, f32[32,896]{1,0:T(8,128)S(1)} %copy-done.39, f32[32,896]{1,0:T(8,128)S(1)} %copy-done.36, f32[32,896]{1,0:T(8,128)S(1)} %copy-done.33), custom_call_target="tpu_custom_call" | custom-call | flops 44040192 | bytes 917504 | tf_op jit(solution)/shard_map/pallas_call | solution.py:393
  154.0 2.0 %copy-done.1 = bf16[2,3584,256]{2,1,0:T(8,128)(2,1)S(1)} copy-done((bf16[2,3584,256]{2,1,0:T(8,128)(2,1)S(1)}, bf16[2,3584,256]{2,1,0:T(8,128)(2,1)}, u32[]{:S(2)}) %copy-start.1) | copy-done | bytes 3670040
  158.8 3.0 %shard_map.105.refs_4_ = bf16[2,4,896,256]{3,2,1,0:T(8,128)(2,1)} custom-call(s32[1]{0:T(128)} %bitcast.me_ref, f32[4,32,896]{2,1,0:T(8,128)S(1)} %shard_map.103.left_ref, f32[32,256]{1,0:T(8,128)S(1)} %shard_map.104.raw_ref, bf16[2,4,896,256]{3,2,1,0:T(8,128)(2,1)S(1)} %bitcast.20, bf16[896,256]{1,0:T(8,128)(2,1)S(1)} %copy-done.23, ...), custom_call_target="tpu_custom_call" | custom-call | flops 176160768 | bytes 5505024 | tf_op jit(solution)/shard_map/pallas_call | solution.py:409
  161.9 3.9 %shard_map.97.left_ref = f32[4,32,896]{2,1,0:T(8,128)S(1)} custom-call(s32[1]{0:T(128)} %bitcast.me_ref, f32[32,896]{1,0:T(8,128)S(1)} %copy-done.47, f32[32,896]{1,0:T(8,128)S(1)} %copy-done.53, f32[32,896]{1,0:T(8,128)S(1)} %copy-done.51, f32[32,896]{1,0:T(8,128)S(1)} %copy-done.49), custom_call_target="tpu_custom_call" | custom-call | flops 44040192 | bytes 917504 | tf_op jit(solution)/shard_map/pallas_call | solution.py:393
  166.9 2.0 %collective-permute-done.25.refs_3_ = bf16[896,256]{1,0:T(8,128)(2,1)S(1)} collective-permute-done((bf16[896,256]{1,0:T(8,128)(2,1)}, bf16[896,256]{1,0:T(8,128)(2,1)S(1)}, u32[]{:S(2)}, u32[]{:S(2)}) %collective-permute-start.25) | collective-permute-done | bytes 458784 | tf_op jit(solution)/shard_map/ppermute | solution.py:391
  173.1 2.0 %shard_map.106 = bf16[2,4,896,256]{3,2,1,0:T(8,128)(2,1)} custom-call(s32[1]{0:T(128)} %bitcast.me_ref, f32[4,32,896]{2,1,0:T(8,128)S(1)} %shard_map.97.left_ref, f32[32,256]{1,0:T(8,128)S(1)} %shard_map.102.raw_ref, bf16[2,4,896,256]{3,2,1,0:T(8,128)(2,1)S(1)} %bitcast.22, bf16[896,256]{1,0:T(8,128)(2,1)S(1)} %copy-done.25, ...), custom_call_target="tpu_custom_call", output_to_operand_aliasing={{}: (8, {})} | custom-call | flops 176160768 | bytes 5505024 | tf_op jit(solution)/shard_map/pallas_call | solution.py:409
  175.1 2.1 %collective-permute-done.26 = f32[2,32,1]{1,0,2:T(2,128)S(1)} collective-permute-done((f32[2,32,1]{1,0,2:T(2,128)S(1)}, f32[2,32,1]{1,0,2:T(2,128)S(1)}, u32[]{:S(2)}, u32[]{:S(2)}) %collective-permute-start.26) | collective-permute-done | bytes 288 | tf_op jit(solution)/shard_map/ppermute | solution.py:425
  (196 shorter events, 61.9 us)
Async XLA Ops:
  9.5 16.3 %collective-permute-start.4 = (bf16[144,896]{1,0:T(8,128)(2,1)S(1)}, bf16[144,896]{1,0:T(8,128)(2,1)S(1)}, u32[]{:S(2)}, u32[]{:S(2)}) collective-permute-start(bf16[144,896]{1,0:T(8,128)(2,1)S(1)} %shard_map.88.refs_0_), channel_id=1, source_target_pairs={{0,56},{4,60},{8,0},{12,4},{16,8},{20,12},{24,16},{28,20},{32,24},... | collective-permute-start | bytes 774152 | tf_op jit(solution)/shard_map/ppermute | solution.py:273
  15.5 10.4 %collective-permute-start.3 = (bf16[144,896]{1,0:T(8,128)(2,1)S(1)}, bf16[144,896]{1,0:T(8,128)(2,1)S(1)}, u32[]{:S(2)}, u32[]{:S(2)}) collective-permute-start(bf16[144,896]{1,0:T(8,128)(2,1)S(1)} %shard_map.88.refs_0_), channel_id=1, source_target_pairs={{0,8},{4,12},{8,16},{12,20},{16,24},{20,28},{24,32},{28,36},{32,40... | collective-permute-start | bytes 774152 | tf_op jit(solution)/shard_map/ppermute | solution.py:273
  18.6 18.1 %collective-permute-start.6 = (bf16[1120,256]{1,0:T(8,128)(2,1)}, bf16[1120,256]{1,0:T(8,128)(2,1)S(1)}, u32[]{:S(2)}, u32[]{:S(2)}) collective-permute-start(bf16[1120,256]{1,0:T(8,128)(2,1)} %get-tuple-element.24.refs_4_.refs_0_.refs_2_), channel_id=1, source_target_pairs={{0,3},{1,0},{2,1},{3,2},{4,7},{5,4},{6,5},{7,6},{8,11},{9,8},{10,9... | collective-permute-start | bytes 1720328 | tf_op jit(solution)/shard_map/ppermute | solution.py:305
  21.7 15.7 %collective-permute-start.5 = (bf16[1120,256]{1,0:T(8,128)(2,1)}, bf16[1120,256]{1,0:T(8,128)(2,1)}, u32[]{:S(2)}, u32[]{:S(2)}) collective-permute-start(bf16[1120,256]{1,0:T(8,128)(2,1)} %get-tuple-element.24.refs_4_.refs_0_.refs_2_), channel_id=1, source_target_pairs={{0,1},{1,2},{2,3},{3,0},{4,5},{5,6},{6,7},{7,4},{8,9},{9,10},{10,1... | collective-permute-start | bytes 1720328 | tf_op jit(solution)/shard_map/ppermute | solution.py:305
  27.9 47.2 %all-to-all-start = ((bf16[8,2,3,16,896]{4,3,2,1,0:T(8,128)(2,1)}), bf16[8,2,3,16,896]{4,3,2,1,0:T(8,128)(2,1)S(1)}, u32[]{:S(2)}, u32[]{:S(2)}) async-start(bf16[8,2,3,16,896]{4,3,2,1,0:T(8,128)(2,1)} %shard_map.89.refs_7_), calls=%async_computation.1 | async-start | bytes 2752512 | tf_op jit(solution)/shard_map/all_to_all | solution.py:356
  32.7 52.3 %reduce-scatter.2.cloned.1.call-start = ((), (), s32[]{:S(2)}) async-start(), calls=%async_computation.4 | async-start | bytes 1146880 | tf_op jit(solution)/shard_map/reduce_scatter | solution.py:314
  33.4 23.9 %collective-permute-start.2 = (bf16[1120,256]{1,0:T(8,128)(2,1)}, bf16[1120,256]{1,0:T(8,128)(2,1)S(1)}, u32[]{:S(2)}, u32[]{:S(2)}) collective-permute-start(bf16[1120,256]{1,0:T(8,128)(2,1)} %get-tuple-element.23.refs_0_.refs_2_), channel_id=1, source_target_pairs={{0,3},{1,0},{2,1},{3,2},{4,7},{5,4},{6,5},{7,6},{8,11},{9,8},{10,9... | collective-permute-start | bytes 1720328 | tf_op jit(solution)/shard_map/ppermute | solution.py:305
  36.7 24.1 %collective-permute-start = (bf16[1120,256]{1,0:T(8,128)(2,1)}, bf16[1120,256]{1,0:T(8,128)(2,1)S(1)}, u32[]{:S(2)}, u32[]{:S(2)}) collective-permute-start(bf16[1120,256]{1,0:T(8,128)(2,1)} %get-tuple-element.23.refs_0_.refs_2_), channel_id=1, source_target_pairs={{0,1},{1,2},{2,3},{3,0},{4,5},{5,6},{6,7},{7,4},{8,9},{9,10},{10,1... | collective-permute-start | bytes 1720328 | tf_op jit(solution)/shard_map/ppermute | solution.py:305
  37.5 9.7 %collective-permute-start.7 = (bf16[144,896]{1,0:T(8,128)(2,1)}, bf16[144,896]{1,0:T(8,128)(2,1)S(1)}, u32[]{:S(2)}, u32[]{:S(2)}) collective-permute-start(bf16[144,896]{1,0:T(8,128)(2,1)} %get-tuple-element.25), channel_id=1, source_target_pairs={{0,8},{4,12},{8,16},{12,20},{16,24},{20,28},{24,32},{28,36},{32,40... | collective-permute-start | bytes 774152 | tf_op jit(solution)/shard_map/ppermute | solution.py:273
  37.5 9.7 %collective-permute-start.8 = (bf16[144,896]{1,0:T(8,128)(2,1)}, bf16[144,896]{1,0:T(8,128)(2,1)S(1)}, u32[]{:S(2)}, u32[]{:S(2)}) collective-permute-start(bf16[144,896]{1,0:T(8,128)(2,1)} %get-tuple-element.26), channel_id=1, source_target_pairs={{0,56},{4,60},{8,0},{12,4},{16,8},{20,12},{24,16},{28,20},{32,24},... | collective-permute-start | bytes 774152 | tf_op jit(solution)/shard_map/ppermute | solution.py:273
  40.8 30.5 %collective-permute-start.13 = (bf16[1120,256]{1,0:T(8,128)(2,1)}, bf16[1120,256]{1,0:T(8,128)(2,1)}, u32[]{:S(2)}, u32[]{:S(2)}) collective-permute-start(bf16[1120,256]{1,0:T(8,128)(2,1)} %get-tuple-element.24.refs_4_.refs_0_.refs_2_), channel_id=1, source_target_pairs={{0,2},{1,3},{2,0},{3,1},{4,6},{5,7},{6,4},{7,5},{8,10},{9,11},{10,... | collective-permute-start | bytes 1720328 | tf_op jit(solution)/shard_map/ppermute | solution.py:305
  47.2 8.6 %collective-permute-start.9 = (bf16[144,896]{1,0:T(8,128)(2,1)S(1)}, bf16[144,896]{1,0:T(8,128)(2,1)S(1)}, u32[]{:S(2)}, u32[]{:S(2)}) collective-permute-start(bf16[144,896]{1,0:T(8,128)(2,1)S(1)} %collective-permute-done.7.refs_0_), channel_id=1, source_target_pairs={{0,8},{4,12},{8,16},{12,20},{16,24},{20,28},{24,32},{28,36},{32,40... | collective-permute-start | bytes 774152 | tf_op jit(solution)/shard_map/ppermute | solution.py:273
  47.2 9.4 %collective-permute-start.10 = (bf16[144,896]{1,0:T(8,128)(2,1)S(1)}, bf16[144,896]{1,0:T(8,128)(2,1)S(1)}, u32[]{:S(2)}, u32[]{:S(2)}) collective-permute-start(bf16[144,896]{1,0:T(8,128)(2,1)S(1)} %collective-permute-done.8.refs_1_), channel_id=1, source_target_pairs={{0,56},{4,60},{8,0},{12,4},{16,8},{20,12},{24,16},{28,20},{32,24},... | collective-permute-start | bytes 774152 | tf_op jit(solution)/shard_map/ppermute | solution.py:273
  62.6 8.8 %collective-permute-start.11 = (bf16[80,896]{1,0:T(8,128)(2,1)S(1)}, bf16[80,896]{1,0:T(8,128)(2,1)S(1)}, u32[]{:S(2)}, u32[]{:S(2)}) collective-permute-start(bf16[80,896]{1,0:T(8,128)(2,1)S(1)} %slice.6), channel_id=1, source_target_pairs={{0,8},{4,12},{8,16},{12,20},{16,24},{20,28},{24,32},{28,36},{32,40... | collective-permute-start | bytes 430088 | tf_op jit(solution)/shard_map/ppermute | solution.py:273
  63.6 7.7 %collective-permute-start.12 = (bf16[64,896]{1,0:T(8,128)(2,1)S(1)}, bf16[64,896]{1,0:T(8,128)(2,1)S(1)}, u32[]{:S(2)}, u32[]{:S(2)}) collective-permute-start(bf16[64,896]{1,0:T(8,128)(2,1)S(1)} %slice.7), channel_id=1, source_target_pairs={{0,56},{4,60},{8,0},{12,4},{16,8},{20,12},{24,16},{28,20},{32,24},... | collective-permute-start | bytes 344072 | tf_op jit(solution)/shard_map/ppermute | solution.py:273
  75.0 20.4 %all-to-all-start.2 = ((bf16[8,1,5,16,896]{4,3,2,1,0:T(8,128)(2,1)}), bf16[8,1,5,16,896]{4,3,2,1,0:T(8,128)(2,1)S(1)}, u32[]{:S(2)}, u32[]{:S(2)}) async-start(bf16[8,1,5,16,896]{4,3,2,1,0:T(8,128)(2,1)} %shard_map.93.refs_8_), calls=%async_computation.3 | async-start | bytes 2293760 | tf_op jit(solution)/shard_map/all_to_all | solution.py:356
  79.9 26.7 %collective-permute-start.1 = (bf16[1120,256]{1,0:T(8,128)(2,1)}, bf16[1120,256]{1,0:T(8,128)(2,1)}, u32[]{:S(2)}, u32[]{:S(2)}) collective-permute-start(bf16[1120,256]{1,0:T(8,128)(2,1)} %get-tuple-element.23.refs_0_.refs_2_), channel_id=1, source_target_pairs={{0,2},{1,3},{2,0},{3,1},{4,6},{5,7},{6,4},{7,5},{8,10},{9,11},{10,... | collective-permute-start | bytes 1720328 | tf_op jit(solution)/shard_map/ppermute | solution.py:305
  96.4 27.0 %all-to-all-start.1 = ((bf16[8,1,5,16,896]{4,3,2,1,0:T(8,128)(2,1)}), bf16[8,1,5,16,896]{4,3,2,1,0:T(8,128)(2,1)S(1)}, u32[]{:S(2)}, u32[]{:S(2)}) async-start(bf16[8,1,5,16,896]{4,3,2,1,0:T(8,128)(2,1)} %copy-done.3), calls=%async_computation.2 | async-start | bytes 2293760 | tf_op jit(solution)/shard_map/all_to_all | solution.py:356
  103.1 10.5 %collective-permute-start.16 = (f32[32,896]{1,0:T(8,128)S(1)}, f32[32,896]{1,0:T(8,128)S(1)}, u32[]{:S(2)}, u32[]{:S(2)}) collective-permute-start(f32[32,896]{1,0:T(8,128)S(1)} %shard_map.95.refs_6_.refs_0_), channel_id=1, source_target_pairs={{0,3},{1,0},{2,1},{3,2},{4,7},{5,4},{6,5},{7,6},{8,11},{9,8},{10,9... | collective-permute-start | bytes 344072 | tf_op jit(solution)/shard_map/ppermute | solution.py:380
  103.2 10.4 %collective-permute-start.15 = (f32[32,896]{1,0:T(8,128)S(1)}, f32[32,896]{1,0:T(8,128)S(1)}, u32[]{:S(2)}, u32[]{:S(2)}) collective-permute-start(f32[32,896]{1,0:T(8,128)S(1)} %shard_map.95.refs_6_.refs_0_), channel_id=1, source_target_pairs={{0,2},{1,3},{2,0},{3,1},{4,6},{5,7},{6,4},{7,5},{8,10},{9,11},{10,... | collective-permute-start | bytes 344072 | tf_op jit(solution)/shard_map/ppermute | solution.py:380
  105.2 8.4 %collective-permute-start.14 = (f32[32,896]{1,0:T(8,128)S(1)}, f32[32,896]{1,0:T(8,128)S(1)}, u32[]{:S(2)}, u32[]{:S(2)}) collective-permute-start(f32[32,896]{1,0:T(8,128)S(1)} %shard_map.95.refs_6_.refs_0_), channel_id=1, source_target_pairs={{0,1},{1,2},{2,3},{3,0},{4,5},{5,6},{6,7},{7,4},{8,9},{9,10},{10,1... | collective-permute-start | bytes 344072 | tf_op jit(solution)/shard_map/ppermute | solution.py:380
  114.4 21.2 %collective-permute-start.20 = (bf16[896,256]{1,0:T(8,128)(2,1)}, bf16[896,256]{1,0:T(8,128)(2,1)S(1)}, u32[]{:S(2)}, u32[]{:S(2)}) collective-permute-start(bf16[896,256]{1,0:T(8,128)(2,1)} %get-tuple-element.36), channel_id=1, source_target_pairs={{0,3},{1,0},{2,1},{3,2},{4,7},{5,4},{6,5},{7,6},{8,11},{9,8},{10,9... | collective-permute-start | bytes 1376264 | tf_op jit(solution)/shard_map/ppermute | solution.py:391
  116.3 25.6 %collective-permute-start.21 = (bf16[896,256]{1,0:T(8,128)(2,1)}, bf16[896,256]{1,0:T(8,128)(2,1)S(1)}, u32[]{:S(2)}, u32[]{:S(2)}) collective-permute-start(bf16[896,256]{1,0:T(8,128)(2,1)} %get-tuple-element.37), channel_id=1, source_target_pairs={{0,2},{1,3},{2,0},{3,1},{4,6},{5,7},{6,4},{7,5},{8,10},{9,11},{10,... | collective-permute-start | bytes 1376264 | tf_op jit(solution)/shard_map/ppermute | solution.py:391
  117.2 24.7 %collective-permute-start.22 = (bf16[896,256]{1,0:T(8,128)(2,1)}, bf16[896,256]{1,0:T(8,128)(2,1)}, u32[]{:S(2)}, u32[]{:S(2)}) collective-permute-start(bf16[896,256]{1,0:T(8,128)(2,1)} %get-tuple-element.38), channel_id=1, source_target_pairs={{0,1},{1,2},{2,3},{3,0},{4,5},{5,6},{6,7},{7,4},{8,9},{9,10},{10,1... | collective-permute-start | bytes 1376264 | tf_op jit(solution)/shard_map/ppermute | solution.py:391
  127.5 14.4 %collective-permute-start.19 = (f32[32,896]{1,0:T(8,128)S(1)}, f32[32,896]{1,0:T(8,128)S(1)}, u32[]{:S(2)}, u32[]{:S(2)}) collective-permute-start(f32[32,896]{1,0:T(8,128)S(1)} %shard_map.96.refs_0_.refs_6_), channel_id=1, source_target_pairs={{0,3},{1,0},{2,1},{3,2},{4,7},{5,4},{6,5},{7,6},{8,11},{9,8},{10,9... | collective-permute-start | bytes 344072 | tf_op jit(solution)/shard_map/ppermute | solution.py:380
  129.4 14.0 %collective-permute-start.18 = (f32[32,896]{1,0:T(8,128)S(1)}, f32[32,896]{1,0:T(8,128)S(1)}, u32[]{:S(2)}, u32[]{:S(2)}) collective-permute-start(f32[32,896]{1,0:T(8,128)S(1)} %shard_map.96.refs_0_.refs_6_), channel_id=1, source_target_pairs={{0,2},{1,3},{2,0},{3,1},{4,6},{5,7},{6,4},{7,5},{8,10},{9,11},{10,... | collective-permute-start | bytes 344072 | tf_op jit(solution)/shard_map/ppermute | solution.py:380
  135.6 8.9 %collective-permute-start.17 = (f32[32,896]{1,0:T(8,128)S(1)}, f32[32,896]{1,0:T(8,128)S(1)}, u32[]{:S(2)}, u32[]{:S(2)}) collective-permute-start(f32[32,896]{1,0:T(8,128)S(1)} %shard_map.96.refs_0_.refs_6_), channel_id=1, source_target_pairs={{0,1},{1,2},{2,3},{3,0},{4,5},{5,6},{6,7},{7,4},{8,9},{9,10},{10,1... | collective-permute-start | bytes 344072 | tf_op jit(solution)/shard_map/ppermute | solution.py:380
  145.2 21.7 %collective-permute-start.23 = (bf16[896,256]{1,0:T(8,128)(2,1)}, bf16[896,256]{1,0:T(8,128)(2,1)S(1)}, u32[]{:S(2)}, u32[]{:S(2)}) collective-permute-start(bf16[896,256]{1,0:T(8,128)(2,1)} %get-tuple-element.39), channel_id=1, source_target_pairs={{0,3},{1,0},{2,1},{3,2},{4,7},{5,4},{6,5},{7,6},{8,11},{9,8},{10,9... | collective-permute-start | bytes 1376264 | tf_op jit(solution)/shard_map/ppermute | solution.py:391
  147.3 19.6 %collective-permute-start.24 = (bf16[896,256]{1,0:T(8,128)(2,1)}, bf16[896,256]{1,0:T(8,128)(2,1)S(1)}, u32[]{:S(2)}, u32[]{:S(2)}) collective-permute-start(bf16[896,256]{1,0:T(8,128)(2,1)} %get-tuple-element.40), channel_id=1, source_target_pairs={{0,2},{1,3},{2,0},{3,1},{4,6},{5,7},{6,4},{7,5},{8,10},{9,11},{10,... | collective-permute-start | bytes 1376264 | tf_op jit(solution)/shard_map/ppermute | solution.py:391
  148.7 20.1 %collective-permute-start.25 = (bf16[896,256]{1,0:T(8,128)(2,1)}, bf16[896,256]{1,0:T(8,128)(2,1)S(1)}, u32[]{:S(2)}, u32[]{:S(2)}) collective-permute-start(bf16[896,256]{1,0:T(8,128)(2,1)} %get-tuple-element.41), channel_id=1, source_target_pairs={{0,1},{1,2},{2,3},{3,0},{4,5},{5,6},{6,7},{7,4},{8,9},{9,10},{10,1... | collective-permute-start | bytes 1376264 | tf_op jit(solution)/shard_map/ppermute | solution.py:391
  169.7 5.4 %collective-permute-start.27 = (f32[2,32,1]{1,0,2:T(2,128)S(1)}, f32[2,32,1]{1,0,2:T(2,128)S(1)}, u32[]{:S(2)}, u32[]{:S(2)}) collective-permute-start(f32[2,32,1]{1,0,2:T(2,128)S(1)} %bitcast.34), channel_id=1, source_target_pairs={{0,2},{1,3},{2,0},{3,1},{4,6},{5,7},{6,4},{7,5},{8,10},{9,11},{10,... | collective-permute-start | bytes 776 | tf_op jit(solution)/shard_map/ppermute | solution.py:425
  172.4 4.8 %collective-permute-start.26 = (f32[2,32,1]{1,0,2:T(2,128)S(1)}, f32[2,32,1]{1,0,2:T(2,128)S(1)}, u32[]{:S(2)}, u32[]{:S(2)}) collective-permute-start(f32[2,32,1]{1,0,2:T(2,128)S(1)} %bitcast.36), channel_id=1, source_target_pairs={{0,1},{1,2},{2,3},{3,0},{4,5},{5,6},{6,7},{7,4},{8,9},{9,10},{10,1... | collective-permute-start | bytes 776 | tf_op jit(solution)/shard_map/ppermute | solution.py:425
  (66 other events, 202.7 us)
Sparse Core Ops, SparseCore 0:
  36.7 36.8 reduce-scatter.1

commit v3 on v2

--- a/solution.py
+++ b/solution.py
@@ -131,6 +131,12 @@
         input_output_aliases={i: i for i in range(len(values))},
         cost_estimate=pl.CostEstimate(flops=0, bytes_accessed=0, transcendentals=0),
     )(*values, *awaited)
+
+
+def halves_kernel(up_ref, down_ref, *refs):
+    upper_ref, lower_ref = refs[-2:]
+    upper_ref[...] = up_ref[: upper_ref.shape[0]]
+    lower_ref[...] = down_ref[upper_ref.shape[0] :]
 
 
 def pack_kernel(tokens_ref, routing_ref, gates_ref, out_ref):
@@ -316,14 +322,21 @@
     blocks = {0: [packed]}
     up = down = packed
     first, last = held
-    gates_at = {1: first[1::2], 3: last[1::2]}
+    gates_at = {1: first[1::2]}
     for k in range(1, along_z // 2):
         up, down = z_shift(up, 1), z_shift(down, -1)
         blocks[k], blocks[-k] = [up], [down]
         if k in gates_at:
             up, down = passing((up, down), gates_at[k])
     half = 80
-    blocks[along_z // 2] = [z_shift(up[:half], 1), z_shift(down[half:], -1)]
+    upper, lower = call(
+        halves_kernel,
+        [jax.ShapeDtypeStruct((count, width), bf16) for count in (half, rows + META - half)],
+        (0, 4 * rows * width),
+        in_specs=[whole(packed.shape)] * 2 + [pl.BlockSpec(memory_space=pl.ANY)] * len(last[1::2]),
+        out_specs=[whole((count, width)) for count in (half, rows + META - half)],
+    )(up, down, *last[1::2])
+    blocks[along_z // 2] = [z_shift(upper, 1), z_shift(lower, -1)]
 
     weights = [
         call(
@@ -334,7 +347,7 @@
         for j in range(local)
     ]
     plan = [(CHUNKS[0], tuple(range(local)), [partial])]
-    plan += [(CHUNKS[1], (0,), first[2:3])]
+    plan += [(CHUNKS[1], (0,), [])]
     plan += [(CHUNKS[1], (1,), [old, weights[0]])]
     arrivals = [[] for _ in range(local)]
     sent = ordered[0]

time: 186 us -> 187 us (level)
  waiting for transfers between devices: 36.3 us -> 43.5 us
  local copies, waits for them, and re-layouts: 36.8 us -> 33.2 us
    ppermute x6, waiting for transfers between devices: 8.38 us -> 20.8 us  [body(): lax.ppermute(ordered[j], 'et', ring(quarters, d))]
    all_to_all x3, waiting for transfers between devices: 5.49 us -> 0.01 us  [body(): lax.all_to_all(sent, 'expert', 0, 0, axis_index_groups=planes, tiled=True)]
    unnamed x132 -> x130, local copies, waits for them, and re-layouts: 33.9 us -> 32.2 us
  transfers between devices with their start and end apart: 33 -> 33, of which waited for: 11 -> 13; matrix products, arithmetic and copies ran while one was open for 2% -> 1% of each run, Pallas kernels for 19% -> 19%
where the time goes in v3:
time: 187 us; the launch traced here: 186 us
  starting transfers between devices  57.9 us (31%)
  waiting for transfers between devices  43.5 us (23%)
  Pallas kernels  36.3 us (19%)
  local copies, waits for them, and re-layouts  33.2 us (18%)
  between operations  14.4 us (8%)
    unnamed x130, local copies, waits for them, and re-layouts  32.2 us
    ppermute x6, waiting for transfers between devices, body(): lax.ppermute(ordered[j], 'et', ring(quarters, d))  20.8 us
    ppermute x8, starting transfers between devices, z_shift(): lax.ppermute(value, 'expert', [(device(x, z, c), device(x, z + step, c))...  15.7 us
    all_to_all x3, starting transfers between devices, body(): lax.all_to_all(sent, 'expert', 0, 0, axis_index_groups=planes, tiled=True)  14.4 us
    ppermute x6, starting transfers between devices, body(): lax.ppermute(ordered[j], 'et', ring(quarters, d))  9.86 us
    ppermute x8, waiting for transfers between devices, z_shift(): lax.ppermute(value, 'expert', [(device(x, z, c), device(x, z + step, c))...  9.53 us
    pallas_call x2, Pallas kernels, body(): call(factor_kernel, jax.ShapeDtypeStruct((quarters, rank, width), f32), (...  7.8 us
    pallas_call x2, Pallas kernels, body(): call(functools.partial(gradient_kernel, len(CHUNKS), quarters), [jax.Shap...  7.68 us
  transfers between devices with their start and end apart: 33, of which 13 were waited for; matrix products, arithmetic and copies ran while one was open for 1% of the time, Pallas kernels for 19%

profile of v3, /device:TPU:2, one launch (start us, length us, event | category | flops | bytes accessed | tf_op | source)
XLA Modules:
  0.0 186.2 jit_solution(12564875439432378433)
XLA Ops:
  9.5 5.9 %collective-permute-start.4 = (bf16[144,896]{1,0:T(8,128)(2,1)S(1)}, bf16[144,896]{1,0:T(8,128)(2,1)S(1)}, u32[]{:S(2)}, u32[]{:S(2)}) collective-permute-start(bf16[144,896]{1,0:T(8,128)(2,1)S(1)} %shard_map.88.refs_0_), channel_id=1, source_target_pairs={{0,56},{4,60},{8,0},{12,4},{16,8},{20,12},{24,16},{28,20},{32,24},... | collective-permute-start | bytes 774152 | tf_op jit(solution)/shard_map/ppermute | solution.py:279
  18.6 3.0 %collective-permute-start.6 = (bf16[1120,256]{1,0:T(8,128)(2,1)}, bf16[1120,256]{1,0:T(8,128)(2,1)S(1)}, u32[]{:S(2)}, u32[]{:S(2)}) collective-permute-start(bf16[1120,256]{1,0:T(8,128)(2,1)} %get-tuple-element.24.refs_4_.refs_0_.refs_2_), channel_id=1, source_target_pairs={{0,3},{1,0},{2,1},{3,2},{4,7},{5,4},{6,5},{7,6},{8,11},{9,8},{10,9... | collective-permute-start | bytes 1720328 | tf_op jit(solution)/shard_map/ppermute | solution.py:311
  21.6 2.0 %copy-done = bf16[2,3584,256]{2,1,0:T(8,128)(2,1)S(1)} copy-done((bf16[2,3584,256]{2,1,0:T(8,128)(2,1)S(1)}, bf16[2,3584,256]{2,1,0:T(8,128)(2,1)}, u32[]{:S(2)}) %copy-start) | copy-done | bytes 3670040
  23.7 2.2 %shard_map.87.refs_3_ = f32[2,32,3584]{2,1,0:T(8,128)} custom-call(f32[2,32,256]{2,1,0:T(8,128)S(1)} %copy-done.61, bf16[2,3584,256]{2,1,0:T(8,128)(2,1)S(1)} %copy-done), custom_call_target="tpu_custom_call" | custom-call | flops 352321536 | bytes 3670016 | tf_op jit(solution)/shard_map/pallas_call | solution.py:314
  25.9 2.0 %shard_map.89.refs_6_ = bf16[8,2,3,16,896]{4,3,2,1,0:T(8,128)(2,1)} custom-call(s32[1]{0:T(128)} %bitcast.1.place_ref, bf16[144,896]{1,0:T(8,128)(2,1)S(1)} %shard_map.88.refs_0_, bf16[144,896]{1,0:T(8,128)(2,1)S(1)} %collective-permute-done.3.refs_1_.refs_0_, bf16[144,896]{1,0:T(8,128)(2,1)S(1)} %collective-permute-done.4.refs_2_.refs_1_, ...), custom_call_target="tpu_custom_call" | custom-call | flops 176160768 | bytes 1376256 | tf_op jit(solution)/shard_map/pallas_call | solution.py:360
  27.8 4.8 %all-to-all-start = ((bf16[8,2,3,16,896]{4,3,2,1,0:T(8,128)(2,1)}), bf16[8,2,3,16,896]{4,3,2,1,0:T(8,128)(2,1)S(1)}, u32[]{:S(2)}, u32[]{:S(2)}) async-start(bf16[8,2,3,16,896]{4,3,2,1,0:T(8,128)(2,1)} %shard_map.89.refs_6_), calls=%async_computation.1 | async-start | bytes 2752512 | tf_op jit(solution)/shard_map/all_to_all | solution.py:369
  33.4 3.3 %collective-permute-start.2 = (bf16[1120,256]{1,0:T(8,128)(2,1)}, bf16[1120,256]{1,0:T(8,128)(2,1)S(1)}, u32[]{:S(2)}, u32[]{:S(2)}) collective-permute-start(bf16[1120,256]{1,0:T(8,128)(2,1)} %get-tuple-element.23.refs_0_.refs_2_), channel_id=1, source_target_pairs={{0,3},{1,0},{2,1},{3,2},{4,7},{5,4},{6,5},{7,6},{8,11},{9,8},{10,9... | collective-permute-start | bytes 1720328 | tf_op jit(solution)/shard_map/ppermute | solution.py:311
  37.5 3.2 %collective-permute-start.8 = (bf16[144,896]{1,0:T(8,128)(2,1)}, bf16[144,896]{1,0:T(8,128)(2,1)S(1)}, u32[]{:S(2)}, u32[]{:S(2)}) collective-permute-start(bf16[144,896]{1,0:T(8,128)(2,1)} %get-tuple-element.26), channel_id=1, source_target_pairs={{0,56},{4,60},{8,0},{12,4},{16,8},{20,12},{24,16},{28,20},{32,24},... | collective-permute-start | bytes 774152 | tf_op jit(solution)/shard_map/ppermute | solution.py:279
  40.8 6.5 %collective-permute-done.7.refs_0_ = bf16[144,896]{1,0:T(8,128)(2,1)S(1)} collective-permute-done((bf16[144,896]{1,0:T(8,128)(2,1)}, bf16[144,896]{1,0:T(8,128)(2,1)S(1)}, u32[]{:S(2)}, u32[]{:S(2)}) %collective-permute-start.7) | collective-permute-done | bytes 258080 | tf_op jit(solution)/shard_map/ppermute | solution.py:279
  47.2 3.2 %collective-permute-start.10 = (bf16[144,896]{1,0:T(8,128)(2,1)S(1)}, bf16[144,896]{1,0:T(8,128)(2,1)S(1)}, u32[]{:S(2)}, u32[]{:S(2)}) collective-permute-start(bf16[144,896]{1,0:T(8,128)(2,1)S(1)} %collective-permute-done.8.refs_1_), channel_id=1, source_target_pairs={{0,56},{4,60},{8,0},{12,4},{16,8},{20,12},{24,16},{28,20},{32,24},... | collective-permute-start | bytes 774152 | tf_op jit(solution)/shard_map/ppermute | solution.py:279
  52.0 4.6 %collective-permute-done.refs_1_.refs_0_.refs_3_ = bf16[1120,256]{1,0:T(8,128)(2,1)S(1)} collective-permute-done((bf16[1120,256]{1,0:T(8,128)(2,1)}, bf16[1120,256]{1,0:T(8,128)(2,1)S(1)}, u32[]{:S(2)}, u32[]{:S(2)}) %collective-permute-start) | collective-permute-done | bytes 573472 | tf_op jit(solution)/shard_map/ppermute | solution.py:311
  56.8 3.2 %collective-permute-start.12 = (bf16[64,896]{1,0:T(8,128)(2,1)S(1)}, bf16[64,896]{1,0:T(8,128)(2,1)S(1)}, u32[]{:S(2)}, u32[]{:S(2)}) collective-permute-start(bf16[64,896]{1,0:T(8,128)(2,1)S(1)} %get-tuple-element.28), channel_id=1, source_target_pairs={{0,56},{4,60},{8,0},{12,4},{16,8},{20,12},{24,16},{28,20},{32,24},... | collective-permute-start | bytes 344072 | tf_op jit(solution)/shard_map/ppermute | solution.py:279
  60.0 2.4 %collective-permute-done.12.refs_5_ = bf16[64,896]{1,0:T(8,128)(2,1)S(1)} collective-permute-done((bf16[64,896]{1,0:T(8,128)(2,1)S(1)}, bf16[64,896]{1,0:T(8,128)(2,1)S(1)}, u32[]{:S(2)}, u32[]{:S(2)}) %collective-permute-start.12) | collective-permute-done | bytes 114720 | tf_op jit(solution)/shard_map/ppermute | solution.py:279
  63.1 2.1 %shard_map.93.refs_8_ = bf16[8,1,5,16,896]{4,3,2,1,0:T(8,128)(2,1)} custom-call(s32[1]{0:T(128)} %bitcast.1.place_ref, bf16[144,896]{1,0:T(8,128)(2,1)S(1)} %collective-permute-done.7.refs_0_, bf16[144,896]{1,0:T(8,128)(2,1)S(1)} %collective-permute-done.8.refs_1_, bf16[144,896]{1,0:T(8,128)(2,1)S(1)} %collective-permute-done.9.up_ref.refs_2_, ...), custom_call_target="tpu_custom_call" | custom-call | flops 146800640 | bytes 1146880 | tf_op jit(solution)/shard_map/pallas_call | solution.py:360
  65.8 4.8 %all-to-all-start.2 = ((bf16[8,1,5,16,896]{4,3,2,1,0:T(8,128)(2,1)}), bf16[8,1,5,16,896]{4,3,2,1,0:T(8,128)(2,1)S(1)}, u32[]{:S(2)}, u32[]{:S(2)}) async-start(bf16[8,1,5,16,896]{4,3,2,1,0:T(8,128)(2,1)} %shard_map.93.refs_8_), calls=%async_computation.3 | async-start | bytes 2293760 | tf_op jit(solution)/shard_map/all_to_all | solution.py:369
  71.4 2.8 %collective-permute-start.1 = (bf16[1120,256]{1,0:T(8,128)(2,1)}, bf16[1120,256]{1,0:T(8,128)(2,1)}, u32[]{:S(2)}, u32[]{:S(2)}) collective-permute-start(bf16[1120,256]{1,0:T(8,128)(2,1)} %get-tuple-element.23.refs_0_.refs_2_), channel_id=1, source_target_pairs={{0,2},{1,3},{2,0},{3,1},{4,6},{5,7},{6,4},{7,5},{8,10},{9,11},{10,... | collective-permute-start | bytes 1720328 | tf_op jit(solution)/shard_map/ppermute | solution.py:311
  74.2 14.0 %collective-permute-done.13.refs_2_.refs_4_ = bf16[1120,256]{1,0:T(8,128)(2,1)S(1)} collective-permute-done((bf16[1120,256]{1,0:T(8,128)(2,1)}, bf16[1120,256]{1,0:T(8,128)(2,1)S(1)}, u32[]{:S(2)}, u32[]{:S(2)}) %collective-permute-start.13) | collective-permute-done | bytes 573472 | tf_op jit(solution)/shard_map/ppermute | solution.py:311
  98.0 4.8 %all-to-all-start.1 = ((bf16[8,1,5,16,896]{4,3,2,1,0:T(8,128)(2,1)}), bf16[8,1,5,16,896]{4,3,2,1,0:T(8,128)(2,1)S(1)}, u32[]{:S(2)}, u32[]{:S(2)}) async-start(bf16[8,1,5,16,896]{4,3,2,1,0:T(8,128)(2,1)} %copy-done.3), calls=%async_computation.2 | async-start | bytes 2293760 | tf_op jit(solution)/shard_map/all_to_all | solution.py:369
  107.4 3.8 %shard_map.99 = (bf16[896,256]{1,0:T(8,128)(2,1)S(1)}, bf16[896,256]{1,0:T(8,128)(2,1)S(1)}, bf16[896,256]{1,0:T(8,128)(2,1)S(1)}, bf16[896,256]{1,0:T(8,128)(2,1)S(1)}) custom-call(bf16[8,2,3,16,896]{4,3,2,1,0:T(8,128)(2,1)S(1)} %all-to-all-done.refs_0_, bf16[8,1,5,16,896]{4,3,2,1,0:T(8,128)(2,1)S(1)} %copy-done.5, ...), custom_call_target="tpu_custom_call" | custom-call | flops 1879048192 | bytes 5505024 | tf_op jit(solution)/shard_map/pallas_call | solution.py:394
  117.4 2.3 %collective-permute-start.21 = (bf16[896,256]{1,0:T(8,128)(2,1)}, bf16[896,256]{1,0:T(8,128)(2,1)S(1)}, u32[]{:S(2)}, u32[]{:S(2)}) collective-permute-start(bf16[896,256]{1,0:T(8,128)(2,1)} %get-tuple-element.37), channel_id=1, source_target_pairs={{0,2},{1,3},{2,0},{3,1},{4,6},{5,7},{6,4},{7,5},{8,10},{9,11},{10,... | collective-permute-start | bytes 1376264 | tf_op jit(solution)/shard_map/ppermute | solution.py:404
  122.0 2.0 %shard_map.86.weights_ref = f32[32,1024]{1,0:T(8,128)S(1)} custom-call(bf16[1120,256]{1,0:T(8,128)(2,1)} %get-tuple-element.23.refs_0_.refs_2_, bf16[1120,256]{1,0:T(8,128)(2,1)S(1)} %copy-done.14, bf16[1120,256]{1,0:T(8,128)(2,1)} %collective-permute-done.1.refs_2_.refs_4_.refs_7_, bf16[1120,256]{1,0:T(8,128)(2,1)S(1)} %copy-done.11), custom_call_target="tpu_custom_call" | custom-call | flops 201326592 | bytes 2097152 | tf_op jit(solution)/shard_map/pallas_call | solution.py:342
  128.8 3.2 %collective-permute-start.19 = (f32[32,896]{1,0:T(8,128)S(1)}, f32[32,896]{1,0:T(8,128)S(1)}, u32[]{:S(2)}, u32[]{:S(2)}) collective-permute-start(f32[32,896]{1,0:T(8,128)S(1)} %shard_map.96.refs_0_.refs_6_), channel_id=1, source_target_pairs={{0,3},{1,0},{2,1},{3,2},{4,7},{5,4},{6,5},{7,6},{8,11},{9,8},{10,9... | collective-permute-start | bytes 344072 | tf_op jit(solution)/shard_map/ppermute | solution.py:393
  132.9 3.8 %shard_map.98 = (bf16[896,256]{1,0:T(8,128)(2,1)S(1)}, bf16[896,256]{1,0:T(8,128)(2,1)S(1)}, bf16[896,256]{1,0:T(8,128)(2,1)S(1)}, bf16[896,256]{1,0:T(8,128)(2,1)S(1)}) custom-call(bf16[8,2,3,16,896]{4,3,2,1,0:T(8,128)(2,1)S(1)} %all-to-all-done.refs_0_, bf16[8,1,5,16,896]{4,3,2,1,0:T(8,128)(2,1)S(1)} %all-to-all-done.1.refs_1_, ...), custom_call_target="tpu_custom_call" | custom-call | flops 1879048192 | bytes 5505024 | tf_op jit(solution)/shard_map/pallas_call | solution.py:394
  139.9 2.2 %collective-permute-done.22.refs_8_.refs_3_ = bf16[896,256]{1,0:T(8,128)(2,1)} collective-permute-done((bf16[896,256]{1,0:T(8,128)(2,1)}, bf16[896,256]{1,0:T(8,128)(2,1)}, u32[]{:S(2)}, u32[]{:S(2)}) %collective-permute-start.22) | collective-permute-done | bytes 458784 | tf_op jit(solution)/shard_map/ppermute | solution.py:404
  142.1 2.4 %collective-permute-done.18.refs_2_.refs_4_ = f32[32,896]{1,0:T(8,128)S(1)} collective-permute-done((f32[32,896]{1,0:T(8,128)S(1)}, f32[32,896]{1,0:T(8,128)S(1)}, u32[]{:S(2)}, u32[]{:S(2)}) %collective-permute-start.18) | collective-permute-done | bytes 114720 | tf_op jit(solution)/shard_map/ppermute | solution.py:393
  146.9 2.0 %collective-permute-start.24 = (bf16[896,256]{1,0:T(8,128)(2,1)}, bf16[896,256]{1,0:T(8,128)(2,1)S(1)}, u32[]{:S(2)}, u32[]{:S(2)}) collective-permute-start(bf16[896,256]{1,0:T(8,128)(2,1)} %get-tuple-element.40), channel_id=1, source_target_pairs={{0,2},{1,3},{2,0},{3,1},{4,6},{5,7},{6,4},{7,5},{8,10},{9,11},{10,... | collective-permute-start | bytes 1376264 | tf_op jit(solution)/shard_map/ppermute | solution.py:404
  149.5 3.9 %shard_map.103.left_ref = f32[4,32,896]{2,1,0:T(8,128)S(1)} custom-call(s32[1]{0:T(128)} %bitcast.me_ref, f32[32,896]{1,0:T(8,128)S(1)} %copy-done.46, f32[32,896]{1,0:T(8,128)S(1)} %copy-done.38, f32[32,896]{1,0:T(8,128)S(1)} %copy-done.35, f32[32,896]{1,0:T(8,128)S(1)} %copy-done.32), custom_call_target="tpu_custom_call" | custom-call | flops 44040192 | bytes 917504 | tf_op jit(solution)/shard_map/pallas_call | solution.py:406
  153.4 2.0 %copy-done.1 = bf16[2,3584,256]{2,1,0:T(8,128)(2,1)S(1)} copy-done((bf16[2,3584,256]{2,1,0:T(8,128)(2,1)S(1)}, bf16[2,3584,256]{2,1,0:T(8,128)(2,1)}, u32[]{:S(2)}) %copy-start.1) | copy-done | bytes 3670040
  158.3 3.0 %shard_map.105.refs_4_ = bf16[2,4,896,256]{3,2,1,0:T(8,128)(2,1)} custom-call(s32[1]{0:T(128)} %bitcast.me_ref, f32[4,32,896]{2,1,0:T(8,128)S(1)} %shard_map.103.left_ref, f32[32,256]{1,0:T(8,128)S(1)} %shard_map.104.raw_ref, bf16[2,4,896,256]{3,2,1,0:T(8,128)(2,1)S(1)} %bitcast.20, bf16[896,256]{1,0:T(8,128)(2,1)S(1)} %copy-done.23, ...), custom_call_target="tpu_custom_call" | custom-call | flops 176160768 | bytes 5505024 | tf_op jit(solution)/shard_map/pallas_call | solution.py:422
  161.3 3.9 %shard_map.97.left_ref = f32[4,32,896]{2,1,0:T(8,128)S(1)} custom-call(s32[1]{0:T(128)} %bitcast.me_ref, f32[32,896]{1,0:T(8,128)S(1)} %copy-done.48, f32[32,896]{1,0:T(8,128)S(1)} %copy-done.54, f32[32,896]{1,0:T(8,128)S(1)} %copy-done.52, f32[32,896]{1,0:T(8,128)S(1)} %copy-done.50), custom_call_target="tpu_custom_call" | custom-call | flops 44040192 | bytes 917504 | tf_op jit(solution)/shard_map/pallas_call | solution.py:406
  166.3 4.1 %collective-permute-done.25.refs_3_ = bf16[896,256]{1,0:T(8,128)(2,1)S(1)} collective-permute-done((bf16[896,256]{1,0:T(8,128)(2,1)}, bf16[896,256]{1,0:T(8,128)(2,1)S(1)}, u32[]{:S(2)}, u32[]{:S(2)}) %collective-permute-start.25) | collective-permute-done | bytes 458784 | tf_op jit(solution)/shard_map/ppermute | solution.py:404
  176.7 2.0 %collective-permute-done.26 = f32[2,32,1]{1,0,2:T(2,128)S(1)} collective-permute-done((f32[2,32,1]{1,0,2:T(2,128)S(1)}, f32[2,32,1]{1,0,2:T(2,128)S(1)}, u32[]{:S(2)}, u32[]{:S(2)}) %collective-permute-start.26) | collective-permute-done | bytes 288 | tf_op jit(solution)/shard_map/ppermute | solution.py:438
  (192 shorter events, 56.2 us)
Async XLA Ops:
  9.5 16.3 %collective-permute-start.4 = (bf16[144,896]{1,0:T(8,128)(2,1)S(1)}, bf16[144,896]{1,0:T(8,128)(2,1)S(1)}, u32[]{:S(2)}, u32[]{:S(2)}) collective-permute-start(bf16[144,896]{1,0:T(8,128)(2,1)S(1)} %shard_map.88.refs_0_), channel_id=1, source_target_pairs={{0,56},{4,60},{8,0},{12,4},{16,8},{20,12},{24,16},{28,20},{32,24},... | collective-permute-start | bytes 774152 | tf_op jit(solution)/shard_map/ppermute | solution.py:279
  15.4 10.4 %collective-permute-start.3 = (bf16[144,896]{1,0:T(8,128)(2,1)S(1)}, bf16[144,896]{1,0:T(8,128)(2,1)S(1)}, u32[]{:S(2)}, u32[]{:S(2)}) collective-permute-start(bf16[144,896]{1,0:T(8,128)(2,1)S(1)} %shard_map.88.refs_0_), channel_id=1, source_target_pairs={{0,8},{4,12},{8,16},{12,20},{16,24},{20,28},{24,32},{28,36},{32,40... | collective-permute-start | bytes 774152 | tf_op jit(solution)/shard_map/ppermute | solution.py:279
  18.6 18.1 %collective-permute-start.6 = (bf16[1120,256]{1,0:T(8,128)(2,1)}, bf16[1120,256]{1,0:T(8,128)(2,1)S(1)}, u32[]{:S(2)}, u32[]{:S(2)}) collective-permute-start(bf16[1120,256]{1,0:T(8,128)(2,1)} %get-tuple-element.24.refs_4_.refs_0_.refs_2_), channel_id=1, source_target_pairs={{0,3},{1,0},{2,1},{3,2},{4,7},{5,4},{6,5},{7,6},{8,11},{9,8},{10,9... | collective-permute-start | bytes 1720328 | tf_op jit(solution)/shard_map/ppermute | solution.py:311
  21.6 15.7 %collective-permute-start.5 = (bf16[1120,256]{1,0:T(8,128)(2,1)}, bf16[1120,256]{1,0:T(8,128)(2,1)}, u32[]{:S(2)}, u32[]{:S(2)}) collective-permute-start(bf16[1120,256]{1,0:T(8,128)(2,1)} %get-tuple-element.24.refs_4_.refs_0_.refs_2_), channel_id=1, source_target_pairs={{0,1},{1,2},{2,3},{3,0},{4,5},{5,6},{6,7},{7,4},{8,9},{9,10},{10,1... | collective-permute-start | bytes 1720328 | tf_op jit(solution)/shard_map/ppermute | solution.py:311
  27.8 38.0 %all-to-all-start = ((bf16[8,2,3,16,896]{4,3,2,1,0:T(8,128)(2,1)}), bf16[8,2,3,16,896]{4,3,2,1,0:T(8,128)(2,1)S(1)}, u32[]{:S(2)}, u32[]{:S(2)}) async-start(bf16[8,2,3,16,896]{4,3,2,1,0:T(8,128)(2,1)} %shard_map.89.refs_6_), calls=%async_computation.1 | async-start | bytes 2752512 | tf_op jit(solution)/shard_map/all_to_all | solution.py:369
  32.7 59.4 %reduce-scatter.2.cloned.1.call-start = ((), (), s32[]{:S(2)}) async-start(), calls=%async_computation.4 | async-start | bytes 1146880 | tf_op jit(solution)/shard_map/reduce_scatter | solution.py:320
  33.4 18.6 %collective-permute-start.2 = (bf16[1120,256]{1,0:T(8,128)(2,1)}, bf16[1120,256]{1,0:T(8,128)(2,1)S(1)}, u32[]{:S(2)}, u32[]{:S(2)}) collective-permute-start(bf16[1120,256]{1,0:T(8,128)(2,1)} %get-tuple-element.23.refs_0_.refs_2_), channel_id=1, source_target_pairs={{0,3},{1,0},{2,1},{3,2},{4,7},{5,4},{6,5},{7,6},{8,11},{9,8},{10,9... | collective-permute-start | bytes 1720328 | tf_op jit(solution)/shard_map/ppermute | solution.py:311
  36.7 19.9 %collective-permute-start = (bf16[1120,256]{1,0:T(8,128)(2,1)}, bf16[1120,256]{1,0:T(8,128)(2,1)S(1)}, u32[]{:S(2)}, u32[]{:S(2)}) collective-permute-start(bf16[1120,256]{1,0:T(8,128)(2,1)} %get-tuple-element.23.refs_0_.refs_2_), channel_id=1, source_target_pairs={{0,1},{1,2},{2,3},{3,0},{4,5},{5,6},{6,7},{7,4},{8,9},{9,10},{10,1... | collective-permute-start | bytes 1720328 | tf_op jit(solution)/shard_map/ppermute | solution.py:311
  37.5 9.7 %collective-permute-start.7 = (bf16[144,896]{1,0:T(8,128)(2,1)}, bf16[144,896]{1,0:T(8,128)(2,1)S(1)}, u32[]{:S(2)}, u32[]{:S(2)}) collective-permute-start(bf16[144,896]{1,0:T(8,128)(2,1)} %get-tuple-element.25), channel_id=1, source_target_pairs={{0,8},{4,12},{8,16},{12,20},{16,24},{20,28},{24,32},{28,36},{32,40... | collective-permute-start | bytes 774152 | tf_op jit(solution)/shard_map/ppermute | solution.py:279
  37.5 9.7 %collective-permute-start.8 = (bf16[144,896]{1,0:T(8,128)(2,1)}, bf16[144,896]{1,0:T(8,128)(2,1)S(1)}, u32[]{:S(2)}, u32[]{:S(2)}) collective-permute-start(bf16[144,896]{1,0:T(8,128)(2,1)} %get-tuple-element.26), channel_id=1, source_target_pairs={{0,56},{4,60},{8,0},{12,4},{16,8},{20,12},{24,16},{28,20},{32,24},... | collective-permute-start | bytes 774152 | tf_op jit(solution)/shard_map/ppermute | solution.py:279
  47.2 9.4 %collective-permute-start.9 = (bf16[144,896]{1,0:T(8,128)(2,1)S(1)}, bf16[144,896]{1,0:T(8,128)(2,1)S(1)}, u32[]{:S(2)}, u32[]{:S(2)}) collective-permute-start(bf16[144,896]{1,0:T(8,128)(2,1)S(1)} %collective-permute-done.7.refs_0_), channel_id=1, source_target_pairs={{0,8},{4,12},{8,16},{12,20},{16,24},{20,28},{24,32},{28,36},{32,40... | collective-permute-start | bytes 774152 | tf_op jit(solution)/shard_map/ppermute | solution.py:279
  47.2 9.4 %collective-permute-start.10 = (bf16[144,896]{1,0:T(8,128)(2,1)S(1)}, bf16[144,896]{1,0:T(8,128)(2,1)S(1)}, u32[]{:S(2)}, u32[]{:S(2)}) collective-permute-start(bf16[144,896]{1,0:T(8,128)(2,1)S(1)} %collective-permute-done.8.refs_1_), channel_id=1, source_target_pairs={{0,56},{4,60},{8,0},{12,4},{16,8},{20,12},{24,16},{28,20},{32,24},... | collective-permute-start | bytes 774152 | tf_op jit(solution)/shard_map/ppermute | solution.py:279
  56.7 6.4 %collective-permute-start.11 = (bf16[80,896]{1,0:T(8,128)(2,1)S(1)}, bf16[80,896]{1,0:T(8,128)(2,1)S(1)}, u32[]{:S(2)}, u32[]{:S(2)}) collective-permute-start(bf16[80,896]{1,0:T(8,128)(2,1)S(1)} %get-tuple-element.27), channel_id=1, source_target_pairs={{0,8},{4,12},{8,16},{12,20},{16,24},{20,28},{24,32},{28,36},{32,40... | collective-permute-start | bytes 430088 | tf_op jit(solution)/shard_map/ppermute | solution.py:279
  56.8 5.6 %collective-permute-start.12 = (bf16[64,896]{1,0:T(8,128)(2,1)S(1)}, bf16[64,896]{1,0:T(8,128)(2,1)S(1)}, u32[]{:S(2)}, u32[]{:S(2)}) collective-permute-start(bf16[64,896]{1,0:T(8,128)(2,1)S(1)} %get-tuple-element.28), channel_id=1, source_target_pairs={{0,56},{4,60},{8,0},{12,4},{16,8},{20,12},{24,16},{28,20},{32,24},... | collective-permute-start | bytes 344072 | tf_op jit(solution)/shard_map/ppermute | solution.py:279
  65.8 31.1 %all-to-all-start.2 = ((bf16[8,1,5,16,896]{4,3,2,1,0:T(8,128)(2,1)}), bf16[8,1,5,16,896]{4,3,2,1,0:T(8,128)(2,1)S(1)}, u32[]{:S(2)}, u32[]{:S(2)}) async-start(bf16[8,1,5,16,896]{4,3,2,1,0:T(8,128)(2,1)} %shard_map.93.refs_8_), calls=%async_computation.3 | async-start | bytes 2293760 | tf_op jit(solution)/shard_map/all_to_all | solution.py:369
  70.6 17.5 %collective-permute-start.13 = (bf16[1120,256]{1,0:T(8,128)(2,1)}, bf16[1120,256]{1,0:T(8,128)(2,1)S(1)}, u32[]{:S(2)}, u32[]{:S(2)}) collective-permute-start(bf16[1120,256]{1,0:T(8,128)(2,1)} %get-tuple-element.24.refs_4_.refs_0_.refs_2_), channel_id=1, source_target_pairs={{0,2},{1,3},{2,0},{3,1},{4,6},{5,7},{6,4},{7,5},{8,10},{9,11},{10,... | collective-permute-start | bytes 1720328 | tf_op jit(solution)/shard_map/ppermute | solution.py:311
  71.4 36.0 %collective-permute-start.1 = (bf16[1120,256]{1,0:T(8,128)(2,1)}, bf16[1120,256]{1,0:T(8,128)(2,1)}, u32[]{:S(2)}, u32[]{:S(2)}) collective-permute-start(bf16[1120,256]{1,0:T(8,128)(2,1)} %get-tuple-element.23.refs_0_.refs_2_), channel_id=1, source_target_pairs={{0,2},{1,3},{2,0},{3,1},{4,6},{5,7},{6,4},{7,5},{8,10},{9,11},{10,... | collective-permute-start | bytes 1720328 | tf_op jit(solution)/shard_map/ppermute | solution.py:311
  98.0 26.7 %all-to-all-start.1 = ((bf16[8,1,5,16,896]{4,3,2,1,0:T(8,128)(2,1)}), bf16[8,1,5,16,896]{4,3,2,1,0:T(8,128)(2,1)S(1)}, u32[]{:S(2)}, u32[]{:S(2)}) async-start(bf16[8,1,5,16,896]{4,3,2,1,0:T(8,128)(2,1)} %copy-done.3), calls=%async_computation.2 | async-start | bytes 2293760 | tf_op jit(solution)/shard_map/all_to_all | solution.py:369
  104.5 9.8 %collective-permute-start.16 = (f32[32,896]{1,0:T(8,128)S(1)}, f32[32,896]{1,0:T(8,128)S(1)}, u32[]{:S(2)}, u32[]{:S(2)}) collective-permute-start(f32[32,896]{1,0:T(8,128)S(1)} %shard_map.95.refs_6_.refs_0_), channel_id=1, source_target_pairs={{0,3},{1,0},{2,1},{3,2},{4,7},{5,4},{6,5},{7,6},{8,11},{9,8},{10,9... | collective-permute-start | bytes 344072 | tf_op jit(solution)/shard_map/ppermute | solution.py:393
  106.4 7.9 %collective-permute-start.15 = (f32[32,896]{1,0:T(8,128)S(1)}, f32[32,896]{1,0:T(8,128)S(1)}, u32[]{:S(2)}, u32[]{:S(2)}) collective-permute-start(f32[32,896]{1,0:T(8,128)S(1)} %shard_map.95.refs_6_.refs_0_), channel_id=1, source_target_pairs={{0,2},{1,3},{2,0},{3,1},{4,6},{5,7},{6,4},{7,5},{8,10},{9,11},{10,... | collective-permute-start | bytes 344072 | tf_op jit(solution)/shard_map/ppermute | solution.py:393
  106.5 8.6 %collective-permute-start.14 = (f32[32,896]{1,0:T(8,128)S(1)}, f32[32,896]{1,0:T(8,128)S(1)}, u32[]{:S(2)}, u32[]{:S(2)}) collective-permute-start(f32[32,896]{1,0:T(8,128)S(1)} %shard_map.95.refs_6_.refs_0_), channel_id=1, source_target_pairs={{0,1},{1,2},{2,3},{3,0},{4,5},{5,6},{6,7},{7,4},{8,9},{9,10},{10,1... | collective-permute-start | bytes 344072 | tf_op jit(solution)/shard_map/ppermute | solution.py:393
  115.7 16.3 %collective-permute-start.20 = (bf16[896,256]{1,0:T(8,128)(2,1)}, bf16[896,256]{1,0:T(8,128)(2,1)S(1)}, u32[]{:S(2)}, u32[]{:S(2)}) collective-permute-start(bf16[896,256]{1,0:T(8,128)(2,1)} %get-tuple-element.36), channel_id=1, source_target_pairs={{0,3},{1,0},{2,1},{3,2},{4,7},{5,4},{6,5},{7,6},{8,11},{9,8},{10,9... | collective-permute-start | bytes 1376264 | tf_op jit(solution)/shard_map/ppermute | solution.py:404
  117.4 22.5 %collective-permute-start.21 = (bf16[896,256]{1,0:T(8,128)(2,1)}, bf16[896,256]{1,0:T(8,128)(2,1)S(1)}, u32[]{:S(2)}, u32[]{:S(2)}) collective-permute-start(bf16[896,256]{1,0:T(8,128)(2,1)} %get-tuple-element.37), channel_id=1, source_target_pairs={{0,2},{1,3},{2,0},{3,1},{4,6},{5,7},{6,4},{7,5},{8,10},{9,11},{10,... | collective-permute-start | bytes 1376264 | tf_op jit(solution)/shard_map/ppermute | solution.py:404
  119.7 22.4 %collective-permute-start.22 = (bf16[896,256]{1,0:T(8,128)(2,1)}, bf16[896,256]{1,0:T(8,128)(2,1)}, u32[]{:S(2)}, u32[]{:S(2)}) collective-permute-start(bf16[896,256]{1,0:T(8,128)(2,1)} %get-tuple-element.38), channel_id=1, source_target_pairs={{0,1},{1,2},{2,3},{3,0},{4,5},{5,6},{6,7},{7,4},{8,9},{9,10},{10,1... | collective-permute-start | bytes 1376264 | tf_op jit(solution)/shard_map/ppermute | solution.py:404
  128.8 13.3 %collective-permute-start.19 = (f32[32,896]{1,0:T(8,128)S(1)}, f32[32,896]{1,0:T(8,128)S(1)}, u32[]{:S(2)}, u32[]{:S(2)}) collective-permute-start(f32[32,896]{1,0:T(8,128)S(1)} %shard_map.96.refs_0_.refs_6_), channel_id=1, source_target_pairs={{0,3},{1,0},{2,1},{3,2},{4,7},{5,4},{6,5},{7,6},{8,11},{9,8},{10,9... | collective-permute-start | bytes 344072 | tf_op jit(solution)/shard_map/ppermute | solution.py:393
  131.9 12.6 %collective-permute-start.18 = (f32[32,896]{1,0:T(8,128)S(1)}, f32[32,896]{1,0:T(8,128)S(1)}, u32[]{:S(2)}, u32[]{:S(2)}) collective-permute-start(f32[32,896]{1,0:T(8,128)S(1)} %shard_map.96.refs_0_.refs_6_), channel_id=1, source_target_pairs={{0,2},{1,3},{2,0},{3,1},{4,6},{5,7},{6,4},{7,5},{8,10},{9,11},{10,... | collective-permute-start | bytes 344072 | tf_op jit(solution)/shard_map/ppermute | solution.py:393
  131.9 13.6 %collective-permute-start.17 = (f32[32,896]{1,0:T(8,128)S(1)}, f32[32,896]{1,0:T(8,128)S(1)}, u32[]{:S(2)}, u32[]{:S(2)}) collective-permute-start(f32[32,896]{1,0:T(8,128)S(1)} %shard_map.96.refs_0_.refs_6_), channel_id=1, source_target_pairs={{0,1},{1,2},{2,3},{3,0},{4,5},{5,6},{6,7},{7,4},{8,9},{9,10},{10,1... | collective-permute-start | bytes 344072 | tf_op jit(solution)/shard_map/ppermute | solution.py:393
  146.2 20.0 %collective-permute-start.23 = (bf16[896,256]{1,0:T(8,128)(2,1)}, bf16[896,256]{1,0:T(8,128)(2,1)S(1)}, u32[]{:S(2)}, u32[]{:S(2)}) collective-permute-start(bf16[896,256]{1,0:T(8,128)(2,1)} %get-tuple-element.39), channel_id=1, source_target_pairs={{0,3},{1,0},{2,1},{3,2},{4,7},{5,4},{6,5},{7,6},{8,11},{9,8},{10,9... | collective-permute-start | bytes 1376264 | tf_op jit(solution)/shard_map/ppermute | solution.py:404
  146.9 19.4 %collective-permute-start.24 = (bf16[896,256]{1,0:T(8,128)(2,1)}, bf16[896,256]{1,0:T(8,128)(2,1)S(1)}, u32[]{:S(2)}, u32[]{:S(2)}) collective-permute-start(bf16[896,256]{1,0:T(8,128)(2,1)} %get-tuple-element.40), channel_id=1, source_target_pairs={{0,2},{1,3},{2,0},{3,1},{4,6},{5,7},{6,4},{7,5},{8,10},{9,11},{10,... | collective-permute-start | bytes 1376264 | tf_op jit(solution)/shard_map/ppermute | solution.py:404
  149.0 21.4 %collective-permute-start.25 = (bf16[896,256]{1,0:T(8,128)(2,1)}, bf16[896,256]{1,0:T(8,128)(2,1)S(1)}, u32[]{:S(2)}, u32[]{:S(2)}) collective-permute-start(bf16[896,256]{1,0:T(8,128)(2,1)} %get-tuple-element.41), channel_id=1, source_target_pairs={{0,1},{1,2},{2,3},{3,0},{4,5},{5,6},{6,7},{7,4},{8,9},{9,10},{10,1... | collective-permute-start | bytes 1376264 | tf_op jit(solution)/shard_map/ppermute | solution.py:404
  171.2 5.4 %collective-permute-start.27 = (f32[2,32,1]{1,0,2:T(2,128)S(1)}, f32[2,32,1]{1,0,2:T(2,128)S(1)}, u32[]{:S(2)}, u32[]{:S(2)}) collective-permute-start(f32[2,32,1]{1,0,2:T(2,128)S(1)} %bitcast.34), channel_id=1, source_target_pairs={{0,2},{1,3},{2,0},{3,1},{4,6},{5,7},{6,4},{7,5},{8,10},{9,11},{10,... | collective-permute-start | bytes 776 | tf_op jit(solution)/shard_map/ppermute | solution.py:438
  173.9 4.8 %collective-permute-start.26 = (f32[2,32,1]{1,0,2:T(2,128)S(1)}, f32[2,32,1]{1,0,2:T(2,128)S(1)}, u32[]{:S(2)}, u32[]{:S(2)}) collective-permute-start(f32[2,32,1]{1,0,2:T(2,128)S(1)} %bitcast.36), channel_id=1, source_target_pairs={{0,1},{1,2},{2,3},{3,0},{4,5},{5,6},{6,7},{7,4},{8,9},{9,10},{10,1... | collective-permute-start | bytes 776 | tf_op jit(solution)/shard_map/ppermute | solution.py:438
  (66 other events, 194.9 us)
Sparse Core Ops, SparseCore 0:
  36.6 26.4 reduce-scatter.1
